TPU v7x, 32 devices: a whole 2x2x4 slice. The times are simulated.
32 devices in a mesh: seq: 8 (over y, x, core), dp: 4 (over z).
Axes of the slice: x: 2, y: 2, z: 4, core: 2. Of those that a mesh axis runs over, the one named last changes fastest.
Arguments:
- queries: bfloat16 [4, 4096, 1024], P('dp', 'seq'), may hold values from -6 to 6
- key_rows: bfloat16 [4, 4096, 1024], P('dp', 'seq'), may hold values from -6 to 6
- value_rows: bfloat16 [4, 4096, 1024], P('dp', 'seq'), may hold values from -6 to 6
- gate_rows: bfloat16 [4, 4096, 1024], P('dp', 'seq'), may hold values from -6 to 6
- cotangent: bfloat16 [4, 4096, 1024], P('dp', 'seq'), may hold values from -6 to 6
- far_blocks: int32 [4, 32, 4], P('dp'), may hold values from 0 to 31, as said below
- treated: int32 [4, 32], P('dp'), may hold values 0 or 1
- norm_gain: float32 [1024], replicated, may hold values from 0.1 to 1.9
- out_weight: bfloat16 [1024, 1024], replicated, may hold values from -0.1875 to 0.1875
Outputs:
- output: bfloat16 [4, 4096, 1024], P('dp', 'seq')
- grad_queries: bfloat16 [4, 4096, 1024], P('dp', 'seq')
- grad_keys: bfloat16 [4, 4096, 1024], P('dp', 'seq')
- grad_values: bfloat16 [4, 4096, 1024], P('dp', 'seq')
- grad_gate: bfloat16 [4, 4096, 1024], P('dp', 'seq')
- grad_weight: float32 [1024, 1024], P(('seq', 'dp'))
- grad_gain: float32 [1024], replicated
Inputs may be any that keep to these rules, and one draw needn't show every extreme that they name: `far_blocks`: every entry names a block of the same history that is held by another index of seq than its query block. Of the 16 entries of the query blocks held by index s of seq, 3 name blocks of index (s + o) mod 8 for o = 1 and o = 2, and 2 for each other o from 3 to 7; which entries these are, and which block of that index, are drawn.
All inputs are finite; a program needn't handle non-finite values. No bound on the sum of `treated` on one device may be relied on, other than what follows from the above.
Results may differ from a plain program's by a relative error of at most 0.0065.
Values may be sent and summed in bfloat16 or wider, within the bound.
A program may use at most 192 MiB of HBM per device.

v0:
```python
import jax
import jax.numpy as jnp
from jax import lax
from jax.sharding import PartitionSpec as P

HEADS = 8
HEAD_DIM = 128
BLK = 128
FAR = 4


epsilon = 1e-05


def from_behind(value, axis, by):
    peers = lax.axis_size(axis)
    pairs = [(i, i + by) for i in range(peers) if 0 <= i + by < peers]
    return lax.ppermute(value, axis, pairs)


def to_heads(rows):
    return rows.reshape(rows.shape[:-1] + (HEADS, rows.shape[-1] // HEADS))


def as_bf16(values):
    return values.astype(jnp.bfloat16)


def pair_scores(query_part, key_part):
    scores = jnp.einsum(
        "pqhd,pkhd->phqk",
        to_heads(query_part),
        to_heads(key_part),
        preferred_element_type=jnp.float32,
    )
    return scores * HEAD_DIM ** (-0.5)


def pair_forward(query_part, key_part, value_part, pair_mask):
    weights = as_bf16(jax.nn.silu(pair_scores(query_part, key_part)) * pair_mask[:, None])
    result = jnp.einsum(
        "phqk,pkhd->pqhd", weights, to_heads(value_part), preferred_element_type=jnp.float32
    )
    return result.reshape(query_part.shape)


def pair_backward(query_part, key_part, value_part, grad_part, pair_mask):
    scores = pair_scores(query_part, key_part)
    logistic = jax.nn.sigmoid(scores)
    weights = as_bf16(jax.nn.silu(scores) * pair_mask[:, None])
    grad_heads = to_heads(grad_part)
    grad_weights = jnp.einsum(
        "pqhd,pkhd->phqk", grad_heads, to_heads(value_part), preferred_element_type=jnp.float32
    )
    grad_value = jnp.einsum(
        "phqk,pqhd->pkhd", weights, grad_heads, preferred_element_type=jnp.float32
    )
    grad_scores = as_bf16(
        grad_weights
        * logistic
        * (1.0 + scores * (1.0 - logistic))
        * pair_mask[:, None]
        * HEAD_DIM ** (-0.5)
    )
    grad_query = jnp.einsum(
        "phqk,pkhd->pqhd", grad_scores, to_heads(key_part), preferred_element_type=jnp.float32
    )
    grad_key = jnp.einsum(
        "phqk,pqhd->pkhd", grad_scores, to_heads(query_part), preferred_element_type=jnp.float32
    )
    row_shape = query_part.shape
    return (
        grad_query.reshape(row_shape),
        grad_key.reshape(row_shape),
        grad_value.reshape(row_shape),
    )


def far_plan(far_all, my_index, seq_count, blocks, capacity):
    block_ids = far_all.reshape(seq_count, blocks * FAR)
    owners = block_ids // blocks
    local_ids = block_ids % blocks
    positions = jnp.arange(blocks * FAR)
    same_owner = owners[:, :, None] == owners[:, None, :]
    before = positions[None, :] < positions[:, None]
    slot_rank = jnp.sum(same_owner & before[None], axis=2)
    slot_ids = jnp.arange(capacity)
    send_hit = (owners[:, None, :] == my_index) & (slot_rank[:, None, :] == slot_ids[None, :, None])
    all_local = jnp.sum(jnp.where(send_hit, local_ids[:, None, :], 0), axis=2).reshape(-1)
    all_ok = jnp.any(send_hit, axis=2).reshape(-1)
    my_owners = lax.dynamic_index_in_dim(owners, my_index, 0, keepdims=False)
    my_ranks = lax.dynamic_index_in_dim(slot_rank, my_index, 0, keepdims=False)
    slot_count = seq_count * capacity
    read_at = my_owners * capacity + my_ranks
    back_hit = read_at[None, :] == jnp.arange(slot_count)[:, None]
    return (all_local, all_ok, read_at, back_hit)


def body(
    queries, key_rows, value_rows, gate_rows, cotangent, far_blocks, treated, norm_gain, out_weight
):
    width = queries.shape[2]
    blocks = queries.shape[1] // BLK
    seq_count = lax.axis_size("seq")
    my_index = lax.axis_index("seq")
    requests = blocks * FAR
    capacity = (requests + seq_count - 2) // (seq_count - 1)
    slot_count = seq_count * capacity
    query_blocks = queries[0].reshape(blocks, BLK, width)
    key_blocks = key_rows[0].reshape(blocks, BLK, width)
    value_blocks = value_rows[0].reshape(blocks, BLK, width)
    both_blocks = jnp.concatenate([key_blocks, value_blocks], axis=2)
    from_prev = from_behind(both_blocks[blocks - 1], "seq", 1)
    prev_both = jnp.concatenate([from_prev[None], both_blocks[:-1]], axis=0)
    prev_keys = prev_both[:, :, :width]
    prev_values = prev_both[:, :, width:]
    causal = jnp.tril(jnp.ones((BLK, BLK), jnp.float32))[None]
    all_ones = jnp.ones((1, BLK, BLK), jnp.float32)
    all_local, all_ok, read_at, back_hit = far_plan(
        far_blocks[0], my_index, seq_count, blocks, capacity
    )
    block_ids = lax.dynamic_slice_in_dim(far_blocks[0], my_index * blocks, blocks, 0).reshape(
        requests
    )
    far_mask = treated[0][block_ids].astype(jnp.float32)[:, None, None]
    far_queries = jnp.repeat(query_blocks, FAR, axis=0)
    back_matrix = back_hit.astype(jnp.bfloat16)
    local_onehot = ((all_local[None, :] == jnp.arange(blocks)[:, None]) & all_ok[None, :]).astype(
        jnp.bfloat16
    )
    diag_out = pair_forward(query_blocks, key_blocks, value_blocks, causal)
    prev_out = pair_forward(query_blocks, prev_keys, prev_values, all_ones)
    send_both = jnp.where(
        all_ok[:, None, None], both_blocks[all_local], jnp.zeros((), jnp.bfloat16)
    )
    got_both = lax.all_to_all(
        send_both.reshape(seq_count, capacity, BLK, 2 * width),
        "seq",
        split_axis=0,
        concat_axis=0,
        tiled=True,
    )
    received = got_both.reshape(slot_count, BLK, 2 * width)
    far_both = received[read_at]
    far_keys = far_both[:, :, :width]
    far_values = far_both[:, :, width:]
    far_terms = as_bf16(pair_forward(far_queries, far_keys, far_values, far_mask))
    far_sum = (
        lax.optimization_barrier(far_terms)
        .astype(jnp.float32)
        .reshape(blocks, FAR, BLK, width)
        .sum(axis=1)
    )
    attention = (diag_out + prev_out + far_sum).reshape(blocks * BLK, width)
    centered = attention - jnp.mean(attention, axis=1, keepdims=True)
    inv_std = lax.rsqrt(jnp.mean(centered * centered, axis=1, keepdims=True) + epsilon)
    normed = centered * inv_std
    gate_vals = gate_rows[0].astype(jnp.float32)
    mixed = as_bf16(normed * norm_gain * gate_vals)
    output = jnp.dot(mixed, out_weight, preferred_element_type=jnp.float32).astype(jnp.bfloat16)
    grad_in = cotangent[0]
    grad_mixed = lax.dot_general(
        grad_in, out_weight, (((1,), (1,)), ((), ())), preferred_element_type=jnp.float32
    )
    grad_weight = lax.psum_scatter(
        lax.dot_general(
            mixed, grad_in, (((0,), (0,)), ((), ())), preferred_element_type=jnp.float32
        ),
        ("seq", "dp"),
        scatter_dimension=0,
        tiled=True,
    )
    grad_gate = as_bf16(grad_mixed * normed * norm_gain)
    scaled = grad_mixed * gate_vals
    grad_gain = lax.psum(jnp.sum(scaled * normed, axis=0), ("seq", "dp"))
    grad_hat = scaled * norm_gain
    grad_attn = inv_std * (
        grad_hat
        - jnp.mean(grad_hat, axis=1, keepdims=True)
        - normed * jnp.mean(grad_hat * normed, axis=1, keepdims=True)
    )
    grad_blocks = as_bf16(grad_attn).reshape(blocks, BLK, width)
    dq_diag, dk_diag, dv_diag = pair_backward(
        query_blocks, key_blocks, value_blocks, grad_blocks, causal
    )
    dq_prev, dk_prev, dv_prev = pair_backward(
        query_blocks, prev_keys, prev_values, grad_blocks, all_ones
    )
    prev_terms = lax.optimization_barrier(as_bf16(jnp.concatenate([dk_prev, dv_prev], axis=2)))
    from_next = from_behind(prev_terms[0], "seq", -1)
    next_terms = jnp.concatenate([prev_terms[1:], from_next[None]], axis=0).astype(jnp.float32)
    far_grads = jnp.repeat(grad_blocks, FAR, axis=0)
    dq_far, dk_far, dv_far = pair_backward(far_queries, far_keys, far_values, far_grads, far_mask)
    query_terms = as_bf16(dq_far)
    back_terms = as_bf16(jnp.concatenate([dk_far, dv_far], axis=2))
    send_back = jnp.dot(
        back_matrix, back_terms.reshape(requests, -1), preferred_element_type=jnp.float32
    )
    send_back = as_bf16(send_back).reshape(slot_count, BLK, 2 * width)
    got_back = lax.all_to_all(
        send_back.reshape(seq_count, capacity, BLK, 2 * width),
        "seq",
        split_axis=0,
        concat_axis=0,
        tiled=True,
    )
    owned_terms = got_back.reshape(slot_count, BLK * 2 * width)
    far_query = (
        lax.optimization_barrier(query_terms)
        .astype(jnp.float32)
        .reshape(blocks, FAR, BLK, width)
        .sum(axis=1)
    )
    owned_sum = jnp.dot(
        local_onehot, lax.optimization_barrier(owned_terms), preferred_element_type=jnp.float32
    )
    owned_sum = owned_sum.reshape(blocks, BLK, 2 * width)
    rows = blocks * BLK
    grad_queries = as_bf16(dq_diag + dq_prev + far_query).reshape(1, rows, width)
    key_total = jnp.concatenate([dk_diag, dv_diag], axis=2) + next_terms + owned_sum
    grad_keys = as_bf16(key_total[:, :, :width]).reshape(1, rows, width)
    grad_values = as_bf16(key_total[:, :, width:]).reshape(1, rows, width)
    return (
        output[None],
        grad_queries,
        grad_keys,
        grad_values,
        grad_gate[None],
        grad_weight,
        grad_gain,
    )


def solution(mesh):
    in_specs = (
        P("dp", "seq", None),
        P("dp", "seq", None),
        P("dp", "seq", None),
        P("dp", "seq", None),
        P("dp", "seq", None),
        P("dp", None, None),
        P("dp", None),
        P(),
        P(),
    )
    out_specs = (
        P("dp", "seq", None),
        P("dp", "seq", None),
        P("dp", "seq", None),
        P("dp", "seq", None),
        P("dp", "seq", None),
        P(("seq", "dp"), None),
        P(),
    )
    return jax.shard_map(body, mesh=mesh, in_specs=in_specs, out_specs=out_specs, check_vma=False)
```

profile of v0, /device:TPU:0, one launch (start us, length us, event | category | flops | bytes accessed | tf_op | source)
XLA Modules:
  0.0 594.1 jit_solution(34854243904092478)
XLA Ops:
  12.2 7.6 %gather_fusion = bf16[24,128,2048]{2,1,0:T(8,128)(2,1)} fusion(bf16[4,128,2048]{2,1,0:T(8,128)(2,1)} %pad_maximum_fusion.1, s32[1024]{0:T(1024)S(1)} %pad_clamp_fusion.2), kind=kCustom, calls=%fused_computation | custom fusion | bytes 25165920 | tf_op jit(solution)/shard_map/gather | solution.py:134
  19.8 10.6 %broadcast_select_fusion = bf16[8,3,128,2048]{3,2,1,0:T(8,128)(2,1)} fusion(bf16[8,3,128,2048]{3,2,1,0:T(8,128)(2,1)} %bitcast.251, pred[8,3]{1,0:T(8,128)(4,1)S(1)} %copy.282), kind=kLoop, calls=%fused_computation.4 | loop fusion | flops 6291456 | bytes 25165848 | tf_op jit(solution)/shard_map/jit(_where)/select_n | solution.py:133
  30.4 5.5 all-to-all-start
  73.0 102.6 %all-to-all-done = bf16[8,3,128,2048]{3,2,1,0:T(8,128)(2,1)} async-done(((bf16[8,3,128,2048]{3,2,1,0:T(8,128)(2,1)}), bf16[8,3,128,2048]{3,2,1,0:T(8,128)(2,1)}, u32[]{:S(2)}, u32[]{:S(2)}) %all-to-all-start) | async-done | bytes 12582944 | tf_op jit(solution)/shard_map/all_to_all | solution.py:136
  175.6 9.5 %gather_fusion.1 = bf16[16,128,2048]{2,1,0:T(8,128)(2,1)} fusion(bf16[24,128,2048]{2,1,0:T(8,128)(2,1)} %bitcast.11, s32[1024]{0:T(1024)S(1)} %pad_clamp_fusion.1), kind=kCustom, calls=%fused_computation.1 | custom fusion | bytes 16777280 | tf_op jit(solution)/shard_map/gather | solution.py:144
  185.1 6.1 %fusion.73 = (bf16[16,128,1024]{2,1,0:T(8,128)(2,1)}, bf16[16,128,1024]{2,1,0:T(8,128)(2,1)}) fusion(bf16[16,128,2048]{2,1,0:T(8,128)(2,1)} %gather_fusion.1), kind=kLoop, calls=%fused_computation.143 | loop fusion | bytes 16777216 | tf_op jit(solution)/shard_map/slice | solution.py:145
  191.1 6.4 %copy.285 = bf16[16,128,1024]{1,2,0:T(8,128)(2,1)} copy(bf16[16,128,1024]{2,1,0:T(8,128)(2,1)} %get-tuple-element.18) | data formatting | bytes 8388608 | tf_op jit(solution)/shard_map/slice | solution.py:145
  197.6 6.3 %copy.284 = bf16[16,128,1024]{1,2,0:T(8,128)(2,1)} copy(bf16[16,128,1024]{2,1,0:T(8,128)(2,1)} %get-tuple-element.19) | data formatting | bytes 8388608 | tf_op jit(solution)/shard_map/slice | solution.py:146
  206.3 5.6 fusion.4
  219.0 5.4 fusion.71
  239.8 5.0 convolution_convert_fusion.1
  244.8 12.7 %fusion.9 = bf16[16,8,128,128]{2,3,1,0:T(8,128)(2,1)} fusion(f32[16,8,128,128]{3,2,1,0:T(8,128)} %get-tuple-element.29, f32[16]{0:T(128)S(1)} %convert_element_type.121, bf16[16,128,8,128]{1,3,2,0:T(8,128)(2,1)} %bitcast.258, bf16[16,128,8,128]{1,3,2,0:T(8,128)(2,1)} %bitcast.261), kind=kOutput, calls=%fused_computation.20 | convolution fusion | flops 562036736 | bytes 20971584 | tf_op jit(solution)/shard_map/pqhd,pkhd->phqk/dot_general | solution.py:52
  257.4 6.7 %copy.315 = bf16[16,128,1024]{2,1,0:T(8,128)(2,1)} copy(bf16[16,128,1024]{1,2,0:T(8,128)(2,1)} %bitcast.263) | data formatting | bytes 8388608 | tf_op jit(solution)/shard_map/reshape | solution.py:75
  264.1 8.4 %convolution_convert_fusion.2 = bf16[16,8,128,128]{2,3,1,0:T(8,128)(2,1)} fusion(bf16[16,8,128,128]{2,3,1,0:T(8,128)(2,1)} %fusion.9, bf16[16,128,8,128]{1,3,2,0:T(8,128)(2,1)} %bitcast.256), kind=kOutput, calls=%fused_computation.26 | convolution fusion | flops 538968064 | bytes 12582912 | tf_op jit(solution)/shard_map/phqk,pqhd->pkhd/dot_general | solution.py:68
  272.5 6.4 %copy.314 = bf16[16,128,1024]{2,1,0:T(8,128)(2,1)} copy(bf16[16,128,1024]{1,2,0:T(8,128)(2,1)} %bitcast.265) | data formatting | bytes 8388608 | tf_op jit(solution)/shard_map/reshape | solution.py:74
  279.0 8.3 %pad_maximum_fusion = bf16[16,128,2048]{2,1,0:T(8,128)(2,1)} fusion(bf16[16,128,1024]{2,1,0:T(8,128)(2,1)} %copy.315, bf16[16,128,1024]{2,1,0:T(8,128)(2,1)} %copy.314), kind=kLoop, calls=%fused_computation.5 | loop fusion | flops 16777216 | bytes 16777216 | tf_op jit(solution)/shard_map/concatenate | solution.py:195
  287.3 11.3 %copy.339 = bf16[2,8,128,2048]{3,1,2,0:T(8,128)(2,1)} copy(bf16[2,8,128,2048]{3,2,1,0:T(8,128)(2,1)} %bitcast.252) | data formatting | bytes 16777216
  298.6 11.4 %convolution_convert_fusion = bf16[24,262144]{1,0:T(8,128)(2,1)} fusion(bf16[16,262144]{1,0:T(8,128)(2,1)} %bitcast.249, s32[16]{0:T(128)S(1)} %bitcast.300), kind=kOutput, calls=%fused_computation.3 | convolution fusion | flops 207618432 | bytes 20971584 | tf_op jit(solution)/shard_map/dot_general | solution.py:196
  309.9 14.7 %copy.340 = bf16[3,8,128,2048]{3,2,1,0:T(8,128)(2,1)} copy(bf16[3,8,128,2048]{3,1,2,0:T(8,128)(2,1)} %bitcast.247) | data formatting | bytes 25165824
  324.6 17.7 %all-to-all-start.1 = ((bf16[8,3,128,2048]{3,2,1,0:T(8,128)(2,1)}), bf16[8,3,128,2048]{3,2,1,0:T(8,128)(2,1)}, u32[]{:S(2)}, u32[]{:S(2)}) async-start(bf16[8,3,128,2048]{3,2,1,0:T(8,128)(2,1)} %bitcast.250), calls=%async_computation.1 | async-start | bytes 25165824 | tf_op jit(solution)/shard_map/all_to_all | solution.py:200
  351.6 4.9 fusion.34
  395.7 147.2 %psum.7 = f32[1024]{0:T(1024)} all-reduce(f32[1024]{0:T(1024)S(1)} %get-tuple-element.7), channel_id=1, replica_groups=mesh['seq'=8,'dp'=4] {'seq','dp'}, use_global_device_ids=true, to_apply=%region_11.12 | all-reduce | flops 1024 | bytes 8192 | tf_op jit(solution)/shard_map/psum | solution.py:175
  552.8 11.7 %copy.341 = bf16[3,8,128,2048]{3,1,2,0:T(8,128)(2,1)S(1)} copy(bf16[3,8,128,2048]{3,2,1,0:T(8,128)(2,1)} %bitcast.95) | data formatting | bytes 25165824
  572.3 5.4 copy.316
  (157 shorter events, 142.1 us)
Async XLA Ops:
  7.2 43.3 %copy-start = (bf16[1024,1024]{1,0:T(8,128)(2,1)S(1)}, bf16[1024,1024]{1,0:T(8,128)(2,1)}, u32[]{:S(2)}) copy-start(bf16[1024,1024]{1,0:T(8,128)(2,1)} %param.17) | copy-start | bytes 6291460
  9.0 3.2 copy-start.30
  30.4 5.5 copy-start.11
  30.4 145.2 %all-to-all-start = ((bf16[8,3,128,2048]{3,2,1,0:T(8,128)(2,1)}), bf16[8,3,128,2048]{3,2,1,0:T(8,128)(2,1)}, u32[]{:S(2)}, u32[]{:S(2)}) async-start(bf16[8,3,128,2048]{3,2,1,0:T(8,128)(2,1)} %broadcast_select_fusion), calls=%async_computation | async-start | bytes 25165824 | tf_op jit(solution)/shard_map/all_to_all | solution.py:136
  35.9 4.9 copy-start.32
  37.7 25.1 %collective-permute-start = (bf16[128,2048]{1,0:T(8,128)(2,1)}, bf16[128,2048]{1,0:T(8,128)(2,1)}, u32[]{:S(2)}, u32[]{:S(2)}) collective-permute-start(bf16[128,2048]{1,0:T(8,128)(2,1)} %fusion.48), channel_id=1, source_target_pairs={{0,4},{4,8},{8,12},{12,16},{16,20},{20,24},{24,28},{1,5},{5,9},{9,... | collective-permute-start | bytes 1572872 | tf_op jit(solution)/shard_map/ppermute | solution.py:18
  45.4 2.8 copy-start.14
  50.4 2.6 copy-start.1
  58.5 4.4 copy-start.19
  203.8 2.5 copy-start.9
  206.0 5.9 copy-start.7
  206.3 5.6 copy-start.10
  224.6 2.9 copy-start.29
  227.5 4.6 copy-start.4
  227.5 4.6 copy-start.12
  237.3 2.5 copy-start.6
  239.4 5.3 copy-start.8
  324.6 228.2 %all-to-all-start.1 = ((bf16[8,3,128,2048]{3,2,1,0:T(8,128)(2,1)}), bf16[8,3,128,2048]{3,2,1,0:T(8,128)(2,1)}, u32[]{:S(2)}, u32[]{:S(2)}) async-start(bf16[8,3,128,2048]{3,2,1,0:T(8,128)(2,1)} %bitcast.250), calls=%async_computation.1 | async-start | bytes 25165824 | tf_op jit(solution)/shard_map/all_to_all | solution.py:200
  342.4 244.5 %reduce-scatter.2.cloned.1.call-start = ((), (), s32[]{:S(2)}) async-start(), calls=%async_computation.3 | async-start | bytes 4325376 | tf_op jit(solution)/shard_map/reduce_scatter | solution.py:165
  368.3 2.3 copy-start.22
  368.3 2.6 copy-start.25
  384.6 193.1 %collective-permute-start.1 = (bf16[128,2048]{0,1:T(8,128)(2,1)}, bf16[128,2048]{0,1:T(8,128)(2,1)}, u32[]{:S(2)}, u32[]{:S(2)}) collective-permute-start(bf16[128,2048]{0,1:T(8,128)(2,1)} %slice_bitcast_fusion), channel_id=1, source_target_pairs={{4,0},{8,4},{12,8},{16,12},{20,16},{24,20},{28,24},{5,1},{9,5},{13... | collective-permute-start | bytes 1572872 | tf_op jit(solution)/shard_map/ppermute | solution.py:18
  542.9 3.1 copy-start.17
  542.9 3.1 copy-start.18
  (14 other events, 23.7 us)
Sparse Core Ops, SparseCore 0:
  356.6 152.3 reduce-scatter.1
where the time goes:
time: 605 us; the launch traced here: 594 us
  local copies, waits for them, and re-layouts  159 us (26%)
  blocking collectives  147 us (24%)
  waiting for transfers between devices  103 us (17%)
  matrix products  89.9 us (15%)
  other arithmetic  52.6 us (9%)
  starting transfers between devices  27.9 us (5%)
  between operations  14.8 us (2%)
    psum x1, blocking collectives, body(): grad_gain = lax.psum(jnp.sum(scaled * normed, axis=0), ('seq', 'dp'))  147 us
    all_to_all x1, waiting for transfers between devices, body(): lax.all_to_all(send_both.reshape(seq_count, capacity, BLK, 2 * width), 's...  103 us
    unnamed x75, local copies, waits for them, and re-layouts  57.6 us
    all_to_all x1, starting transfers between devices, body(): lax.all_to_all(send_back.reshape(seq_count, capacity, BLK, 2 * width), 's...  17.7 us
    dot_general x3, matrix products, pair_backward(): jnp.einsum('pqhd,pkhd->phqk', grad_heads, to_heads(value_part), preferred...  17.5 us
    slice x2, local copies, waits for them, and re-layouts, body(): far_keys = far_both[:, :, :width]  12.5 us
  transfers between devices with their start and end apart: 5, of which 1 were waited for; matrix products, arithmetic and copies ran while one was open for 21% of the time, Pallas kernels for 0%

commit v1 on v0

v1 whole, which is shorter than its diff:
```python
import functools

import jax
import jax.numpy as jnp
from jax import lax
from jax.experimental import pallas as pl
from jax.experimental.pallas import tpu as pltpu
from jax.sharding import PartitionSpec as P

HEADS = 8
HEAD_DIM = 128
BLK = 128
FAR = 4
EPS = 1e-05
SCALE = HEAD_DIM ** (-0.5)
NT = (((1,), (1,)), ((), ()))
TN = (((0,), (0,)), ((), ()))


def dot(a, b, dims=(((1,), (0,)), ((), ()))):
    return lax.dot_general(a, b, dims, preferred_element_type=jnp.float32)


def silu_parts(raw):
    half = raw * (0.5 * SCALE)
    t = jnp.tanh(half)
    act = half + half * t
    sig = 0.5 + 0.5 * t
    return act, sig + act * (1.0 - sig)


def query_kernel(
    nb, far_s, treated_s, my_s, q_ref, k0, v0, k1, v1, k2, v2, k3, v3, k4, v4, k5, v5,
    gate_ref, cot_ref, gain_ref, w_ref,
    out_ref, dq_ref, dgate_ref, mixed_ref, c_ref, dgain_ref, att, slope,
):
    i = pl.program_id(0)
    block = my_s[0] * nb + i
    keys = (k0, k1, k2, k3, k4, k5)
    vals = (v0, v1, v2, v3, v4, v5)
    flags = [None, (block > 0).astype(jnp.float32)]
    flags += [treated_s[far_s[block * FAR + f]].astype(jnp.float32) for f in range(FAR)]
    row = lax.broadcasted_iota(jnp.int32, (BLK, BLK), 0)
    col = lax.broadcasted_iota(jnp.int32, (BLK, BLK), 1)
    tril = (row >= col).astype(jnp.float32)
    for h in range(HEADS):
        hs = slice(h * HEAD_DIM, (h + 1) * HEAD_DIM)
        q = q_ref[:, hs]
        acts = []
        for p in range(2 + FAR):
            act, der = silu_parts(dot(q, keys[p][:, hs], NT))
            m = tril if p == 0 else flags[p]
            acts.append((act * m).astype(jnp.bfloat16))
            slope[h, :, p * BLK : (p + 1) * BLK] = der * m
        att[:, hs] = dot(
            jnp.concatenate(acts, axis=1), jnp.concatenate([v[:, hs] for v in vals], axis=0)
        )
    attention = att[...]
    centered = attention - jnp.mean(attention, axis=1, keepdims=True)
    inv_std = lax.rsqrt(jnp.mean(centered * centered, axis=1, keepdims=True) + EPS)
    normed = centered * inv_std
    gate = gate_ref[...].astype(jnp.float32)
    gain = gain_ref[...]
    mixed = (normed * gain * gate).astype(jnp.bfloat16)
    mixed_ref[...] = mixed
    out_ref[...] = dot(mixed, w_ref[...]).astype(jnp.bfloat16)
    gm = dot(cot_ref[...], w_ref[...], NT)
    dgate_ref[...] = (gm * normed * gain).astype(jnp.bfloat16)
    scaled = gm * gate
    part = jnp.sum(scaled * normed, axis=0, keepdims=True)

    @pl.when(i == 0)
    def _():
        dgain_ref[...] = part

    @pl.when(i > 0)
    def _():
        dgain_ref[...] += part

    g = scaled * gain
    c = inv_std * (
        g - jnp.mean(g, axis=1, keepdims=True)
        - normed * jnp.mean(g * normed, axis=1, keepdims=True)
    )
    c_ref[...] = c.astype(jnp.bfloat16)
    for h in range(HEADS):
        hs = slice(h * HEAD_DIM, (h + 1) * HEAD_DIM)
        ch = c_ref[:, hs]
        ds = []
        for p in range(2 + FAR):
            da = dot(ch, vals[p][:, hs], NT)
            ds.append((da * slope[h, :, p * BLK : (p + 1) * BLK]).astype(jnp.bfloat16))
        dq = dot(
            jnp.concatenate(ds, axis=1), jnp.concatenate([k[:, hs] for k in keys], axis=0)
        )
        dq_ref[:, hs] = (dq * SCALE).astype(jnp.bfloat16)


def key_kernel(
    steps, qi_s, ki_s, on_s, q_ref, c_ref, k_ref, v_ref, dk_ref, dv_ref, dk_acc, dv_acc
):
    r = pl.program_id(0)

    @pl.when(r == 0)
    def _():
        dk_acc[...] = jnp.zeros_like(dk_acc)
        dv_acc[...] = jnp.zeros_like(dv_acc)

    at = pl.ds(pl.multiple_of(ki_s[r] * BLK, BLK), BLK)
    mode = on_s[r]
    on = (mode > 0).astype(jnp.float32)
    off_diag = jnp.where(mode == 2, 0.0, on)
    row = lax.broadcasted_iota(jnp.int32, (BLK, BLK), 0)
    col = lax.broadcasted_iota(jnp.int32, (BLK, BLK), 1)
    m = jnp.where(col >= row, on, off_diag)
    for h in range(HEADS):
        hs = slice(h * HEAD_DIM, (h + 1) * HEAD_DIM)
        q = q_ref[:, hs]
        c = c_ref[:, hs]
        act, der = silu_parts(dot(k_ref[at, hs], q, NT))
        da = dot(v_ref[at, hs], c, NT)
        dv_acc[at, hs] += dot((act * m).astype(jnp.bfloat16), c)
        dk_acc[at, hs] += dot((da * der * m).astype(jnp.bfloat16), q)

    @pl.when(r == steps - 1)
    def _():
        dk_ref[...] = (dk_acc[...] * SCALE).astype(jnp.bfloat16)
        dv_ref[...] = dv_acc[...].astype(jnp.bfloat16)


def run_query(q, k, v, k_all, v_all, gate, cot, far, treated, me, gain, w):
    rows, width = q.shape
    nb = rows // BLK
    shape = (BLK, width)
    own = pl.BlockSpec(shape, lambda i, far, tr, my: (i, 0))
    prev = pl.BlockSpec(shape, lambda i, far, tr, my: (jnp.maximum(my[0] * nb + i - 1, 0), 0))

    def listed(f):
        return pl.BlockSpec(shape, lambda i, far, tr, my: (far[(my[0] * nb + i) * FAR + f], 0))

    kv_specs = [own, own, prev, prev]
    kv = [k, v, k_all, v_all]
    for f in range(FAR):
        kv_specs += [listed(f)] * 2
        kv += [k_all, v_all]
    whole = pl.BlockSpec((width, width), lambda i, far, tr, my: (0, 0))
    vec = pl.BlockSpec((1, width), lambda i, far, tr, my: (0, 0))
    big = jax.ShapeDtypeStruct((rows, width), jnp.bfloat16)
    return pl.pallas_call(
        functools.partial(query_kernel, nb),
        out_shape=(big, big, big, big, big, jax.ShapeDtypeStruct((1, width), jnp.float32)),
        grid_spec=pltpu.PrefetchScalarGridSpec(
            num_scalar_prefetch=3,
            grid=(nb,),
            in_specs=[own] + kv_specs + [own, own, vec, whole],
            out_specs=(own, own, own, own, own, vec),
            scratch_shapes=[
                pltpu.VMEM((BLK, width), jnp.float32),
                pltpu.VMEM((HEADS, BLK, (2 + FAR) * BLK), jnp.float32),
            ],
        ),
        compiler_params=pltpu.CompilerParams(vmem_limit_bytes=40 * 2**20),
        cost_estimate=pl.CostEstimate(
            flops=8 * 10**9, bytes_accessed=24 * 2**20, transcendentals=3 * 10**6
        ),
        name="query_side",
    )(far, treated, me, q, *kv, gate, cot, gain, w)


def run_keys(qi, ki, on, q_all, c_all, k, v):
    rows, width = k.shape
    steps = qi.shape[0]
    pick = pl.BlockSpec((BLK, width), lambda r, qi, ki, on: (qi[r], 0))
    whole = pl.BlockSpec((rows, width), lambda r, qi, ki, on: (0, 0))
    big = jax.ShapeDtypeStruct((rows, width), jnp.bfloat16)
    return pl.pallas_call(
        functools.partial(key_kernel, steps),
        out_shape=(big, big),
        grid_spec=pltpu.PrefetchScalarGridSpec(
            num_scalar_prefetch=3,
            grid=(steps,),
            in_specs=[pick, pick, whole, whole],
            out_specs=(whole, whole),
            scratch_shapes=[pltpu.VMEM((rows, width), jnp.float32)] * 2,
        ),
        compiler_params=pltpu.CompilerParams(vmem_limit_bytes=40 * 2**20),
        cost_estimate=pl.CostEstimate(
            flops=4 * 10**9, bytes_accessed=16 * 2**20, transcendentals=3 * 10**6
        ),
        name="key_side",
    )(qi, ki, on, q_all, c_all, k, v)


def key_plan(far, treated, me, nb):
    total = far.shape[0]
    mine = (far // nb) == me
    ids = jnp.arange(total)
    rank = jnp.sum((ids[None, :] < ids[:, None]) & mine[None, :], axis=1)
    hit = mine[None, :] & (rank[None, :] == jnp.arange(nb * FAR)[:, None])
    flag = jnp.sum(
        jnp.where(far[:, None] == jnp.arange(treated.shape[0])[None, :], treated[None, :], 0),
        axis=1,
    )

    def take(values):
        return jnp.sum(jnp.where(hit, values[None, :], 0), axis=1)

    local = jnp.arange(nb)
    after = me * nb + local + 1
    last = treated.shape[0] - 1
    qi = jnp.concatenate([me * nb + local, jnp.minimum(after, last), take(ids // FAR)])
    ki = jnp.concatenate([local, local, take(far % nb)])
    on = jnp.concatenate(
        [jnp.full((nb,), 2), (after <= last).astype(jnp.int32), take(flag)]
    )
    return qi.astype(jnp.int32), ki.astype(jnp.int32), on.astype(jnp.int32)


def gather(rows):
    return lax.all_gather(rows, "seq", axis=0, tiled=True)


def body(q, k, v, gate, cot, far_blocks, treated, gain, w):
    q, k, v, gate, cot = q[0], k[0], v[0], gate[0], cot[0]
    rows, width = q.shape
    nb = rows // BLK
    me = lax.axis_index("seq").astype(jnp.int32)
    far = far_blocks[0].reshape(-1)
    flags = treated[0]
    k_all, v_all = gather(k), gather(v)
    q_all = gather(q)
    out, dq, dgate, mixed, c, dgain = run_query(
        q, k, v, k_all, v_all, gate, cot, far, flags, me[None], gain[None], w
    )
    c_all = gather(c)
    grad_weight = dot(mixed, cot, TN)
    seqs, dps = lax.axis_size("seq"), lax.axis_size("dp")
    grad_weight = grad_weight.reshape(seqs, dps, -1, width)
    grad_weight = lax.psum_scatter(grad_weight, "dp", scatter_dimension=1, tiled=False)
    grad_weight = lax.psum_scatter(grad_weight, "seq", scatter_dimension=0, tiled=False)
    dgain = lax.psum(dgain[0], ("seq", "dp"))
    qi, ki, on = key_plan(far, flags, me, nb)
    dk, dv = run_keys(qi, ki, on, q_all, c_all, k, v)
    return out[None], dq[None], dk[None], dv[None], dgate[None], grad_weight, dgain


def solution(mesh):
    big = P("dp", "seq", None)
    in_specs = (big,) * 5 + (P("dp", None, None), P("dp", None), P(), P())
    out_specs = (big,) * 5 + (P(("seq", "dp"), None), P())
    return jax.shard_map(body, mesh=mesh, in_specs=in_specs, out_specs=out_specs, check_vma=False)
```

time: 605 us -> 483 us (0.80); the launches traced: 594 us -> 483 us
  waiting for transfers between devices: 103 us -> 339 us
  local copies, waits for them, and re-layouts: 159 us -> 17.4 us
  blocking collectives: 147 us -> 39.7 us
  matrix products: 89.9 us -> 3.22 us
  Pallas kernels: 0 us -> 67.9 us
  other arithmetic: 52.6 us -> 0.54 us
  starting transfers between devices: 27.9 us -> 0.23 us
    all_gather x0 -> x4, waiting for transfers between devices: none -> 184 us  [gather(): return lax.all_gather(rows, 'seq', axis=0, tiled=True)]
    unnamed x1 -> x7, waiting for transfers between devices: 0.02 us -> 156 us
    psum x1, blocking collectives: 147 us -> 39.7 us  [body(): dgain = lax.psum(dgain[0], ('seq', 'dp'))]
    all_to_all x2 -> x0, waiting for transfers between devices: 103 us -> none  [the longest x1 103 us: body(): lax.all_to_all(send_both.reshape(seq_count, capacity, BLK, 2 * width), 's...]
    dot_general x23 -> x1, matrix products: 89.9 us -> 3.22 us  [dot(): return lax.dot_general(a, b, dims, preferred_element_type=jnp.float32)]
    pallas_call x0 -> x2, Pallas kernels: none -> 67.9 us  [the longest x1 39.5 us: run_keys(): pl.pallas_call(functools.partial(key_kernel, steps), out_shape=(big, big)...]
    unnamed x75 -> x30, local copies, waits for them, and re-layouts: 57.6 us -> 13.8 us
    slice x9 -> x0, local copies, waits for them, and re-layouts: 30.6 us -> none  [the longest x2 12.5 us: body(): far_keys = far_both[:, :, :width]]
  transfers between devices with their start and end apart: 5 -> 6, of which waited for: 1 -> 5; matrix products, arithmetic and copies ran while one was open for 21% -> 1% of each run, Pallas kernels for 0% -> 8%
where the time goes in v1:
time: 483 us
  waiting for transfers between devices  339 us (70%)
  Pallas kernels  67.9 us (14%)
  blocking collectives  39.7 us (8%)
  local copies, waits for them, and re-layouts  17.4 us (4%)
  between operations  14.2 us (3%)
    all_gather x4, waiting for transfers between devices, gather(): return lax.all_gather(rows, 'seq', axis=0, tiled=True)  184 us
    unnamed x7, waiting for transfers between devices  156 us
    psum x1, blocking collectives, body(): dgain = lax.psum(dgain[0], ('seq', 'dp'))  39.7 us
    pallas_call x1, Pallas kernels, run_keys(): pl.pallas_call(functools.partial(key_kernel, steps), out_shape=(big, big)...  39.5 us
    pallas_call x1, Pallas kernels, run_query(): pl.pallas_call(functools.partial(query_kernel, nb), out_shape=(big, big,...  28.4 us
    unnamed x30, local copies, waits for them, and re-layouts  13.8 us
  transfers between devices with their start and end apart: 6, of which 5 were waited for; matrix products, arithmetic and copies ran while one was open for 1% of the time, Pallas kernels for 8%

profile of v1, /device:TPU:0, one launch (start us, length us, event | category | flops | bytes accessed | tf_op | source)
XLA Modules:
  0.0 482.6 jit_solution(16020593451573492447)
XLA Ops:
  7.2 0.7 all-gather.10.cloned.1.call-update
  7.9 0.7 all-gather.12.cloned.1.call-update
  8.7 0.8 copy.22
  9.6 57.4 %all-gather.10.cloned.1.call-done = bf16[1,4096,1024]{2,1,0:T(8,128)(2,1)} async-done(((bf16[1,512,1024]{2,1,0:T(8,128)(2,1)}), bf16[1,4096,1024]{2,1,0:T(8,128)(2,1)}) %all-gather.10.cloned.1.call-update) | async-done | bytes 8388624 | tf_op jit(solution)/shard_map/all_gather | solution.py:220
  67.0 56.3 %all-gather.12.cloned.1.call-done = bf16[1,4096,1024]{2,1,0:T(8,128)(2,1)} async-done(((bf16[1,512,1024]{2,1,0:T(8,128)(2,1)}), bf16[1,4096,1024]{2,1,0:T(8,128)(2,1)}) %all-gather.12.cloned.1.call-update) | async-done | bytes 8388624 | tf_op jit(solution)/shard_map/all_gather | solution.py:220
  123.3 1.2 copy-done
  124.5 1.2 copy-done.2
  125.8 1.2 copy-done.5
  127.0 1.2 copy-done.6
  128.2 1.6 copy-done.8
  129.8 1.2 copy-done.9
  131.0 0.7 copy-done.10
  131.7 0.7 copy-done.11
  132.4 28.4 %query_side.1 = (bf16[512,1024]{1,0:T(8,128)(2,1)}, bf16[512,1024]{1,0:T(8,128)(2,1)}, bf16[512,1024]{1,0:T(8,128)(2,1)}, bf16[512,1024]{1,0:T(8,128)(2,1)S(1)},...) custom-call(s32[128]{0:T(128)S(1)} %reshape_squeeze.3.far_s, s32[32]{0:T(128)S(1)} %bitcast.47, s32[1]{0:T(128)} %bitcast.1.my_s, ...), custom_call_target="tpu_custom_call" | custom-call | flops 8000000000 | bytes 25165824 | tf_op jit(solution)/shard_map/query_side/pallas_call | solution.py:149
  160.8 0.5 copy.23
  161.4 3.2 fusion
  165.9 0.6 dynamic-slice
  166.5 153.3 %all-reduce.3.cloned.1.call-done = f32[8,4,32,1024]{3,2,1,0:T(8,128)} async-done(((f32[8,4,32,1024]{3,2,1,0:T(8,128)}), f32[8,4,32,1024]{3,2,1,0:T(8,128)}) %all-reduce.3.cloned.1.call-update) | async-done | bytes 4194320
  319.8 3.0 dynamic-slice_bitcast_fusion
  323.3 39.7 %psum.7 = f32[1024]{0:T(1024)} all-reduce(f32[1024]{0:T(1024)S(1)} %bitcast.46), channel_id=1, replica_groups=mesh['seq'=8,'dp'=4] {'seq','dp'}, use_global_device_ids=true, to_apply=%region_7.8 | all-reduce | flops 1024 | bytes 8192 | tf_op jit(solution)/shard_map/psum | solution.py:241
  363.0 13.0 %all-gather.14.cloned.1.call-done = bf16[1,4096,1024]{2,1,0:T(8,128)(2,1)} async-done(((bf16[1,512,1024]{2,1,0:T(8,128)(2,1)}), bf16[1,4096,1024]{2,1,0:T(8,128)(2,1)}) %all-gather.14.cloned.1.call-update) | async-done | bytes 8388624 | tf_op jit(solution)/shard_map/all_gather | solution.py:220
  376.0 56.9 %all-gather.8.cloned.1.call-done.c_ref = bf16[4096,1024]{1,0:T(8,128)(2,1)} async-done(((bf16[512,1024]{1,0:T(8,128)(2,1)}), bf16[4096,1024]{1,0:T(8,128)(2,1)}) %all-gather.8.cloned.1.call-update) | async-done | bytes 8388624 | tf_op jit(solution)/shard_map/all_gather | solution.py:220
  432.9 3.4 copy-done.4
  436.3 39.5 %key_side.1 = (bf16[512,1024]{1,0:T(8,128)(2,1)}, bf16[512,1024]{1,0:T(8,128)(2,1)}) custom-call(s32[24]{0:T(128)S(1)} %get-tuple-element.26.qi_s, s32[24]{0:T(128)S(1)} %get-tuple-element.27.ki_s, s32[24]{0:T(128)S(1)} %pad_add_fusion.2.on_s, bf16[4096,1024]{1,0:T(8,128)(2,1)S(1)} %bitcast.40, bf16[4096,1024]{1,0:T(8,128)(2,1)} %all-gather.8.cloned.1.call-done.c_ref, ...), custom_call_target="tpu_custom_call" | custom-call | flops 4000000000 | bytes 16777216 | tf_op jit(solution)/shard_map/key_side/pallas_call | solution.py:176
  (44 shorter events, 2.0 us)
Async XLA Ops:
  7.2 59.8 %all-gather.10.cloned.1.call-start = ((), (), s32[]{:S(2)}) async-start(), calls=%async_computation.3 | async-start | bytes 9437184 | tf_op jit(solution)/shard_map/all_gather | solution.py:220
  7.9 115.4 %all-gather.12.cloned.1.call-start = ((), (), s32[]{:S(2)}) async-start(), calls=%async_computation.4 | async-start | bytes 9437184 | tf_op jit(solution)/shard_map/all_gather | solution.py:220
  8.6 311.1 %all-reduce.3.cloned.1.call-start = ((), (), s32[]{:S(2)}) async-start(), calls=%async_computation.6 | async-start | bytes 8388608
  123.3 1.2 copy-start
  124.5 1.2 copy-start.2
  125.8 1.2 copy-start.5
  127.0 1.2 copy-start.6
  128.2 1.6 copy-start.8
  129.8 1.2 copy-start.9
  131.0 0.7 copy-start.10
  131.7 0.7 copy-start.11
  132.4 29.0 %copy-start.7 = (bf16[1,512,1024]{2,1,0:T(8,128)(2,1)S(1)}, bf16[1,512,1024]{2,1,0:T(8,128)(2,1)}, u32[]{:S(2)}) copy-start(bf16[1,512,1024]{2,1,0:T(8,128)(2,1)} %param.13) | copy-start | bytes 3145732
  164.6 1.3 copy-start.13
  164.6 158.3 %copy-start.12 = (s32[1,32]{1,0:T(1,128)S(1)}, s32[1,32]{1,0:T(1,128)}, u32[]{:S(2)}) copy-start(s32[1,32]{1,0:T(1,128)} %param.15) | copy-start | bytes 388
  164.6 268.3 %copy-start.1 = (bf16[1,512,1024]{2,1,0:T(8,128)(2,1)S(1)}, bf16[1,512,1024]{2,1,0:T(8,128)(2,1)}, u32[]{:S(2)}) copy-start(bf16[1,512,1024]{2,1,0:T(8,128)(2,1)} %param.10) | copy-start | bytes 3145732
  164.6 268.3 %copy-start.3 = (bf16[1,512,1024]{2,1,0:T(8,128)(2,1)S(1)}, bf16[1,512,1024]{2,1,0:T(8,128)(2,1)}, u32[]{:S(2)}) copy-start(bf16[1,512,1024]{2,1,0:T(8,128)(2,1)} %param.11) | copy-start | bytes 3145732
  164.6 211.4 %all-gather.14.cloned.1.call-start = ((), (), s32[]{:S(2)}) async-start(), calls=%async_computation.5 | async-start | bytes 9437184 | tf_op jit(solution)/shard_map/all_gather | solution.py:220
  165.2 267.7 %all-gather.8.cloned.1.call-start = ((), (), s32[]{:S(2)}) async-start(), calls=%async_computation.1 | async-start | bytes 9437184 | tf_op jit(solution)/shard_map/all_gather | solution.py:220
  165.8 309.9 %reduce-scatter.5.cloned.1.call-start = ((), (), s32[]{:S(2)}) async-start(), calls=%async_computation.2 | async-start | bytes 1179648 | tf_op jit(solution)/shard_map/reduce_scatter | solution.py:240
  432.9 3.4 copy-start.4
Sparse Core Ops, SparseCore 0:
  9.9 57.0 all-gather.9
  68.9 54.3 all-gather.11
  164.7 154.9 all-reduce.2
  321.7 54.2 all-gather.13
  378.5 54.3 all-gather.7
  436.8 36.2 reduce-scatter.4

commit v2 on v1

--- a/solution.py
+++ b/solution.py
@@ -12,6 +12,8 @@
 BLK = 128
 FAR = 4
 EPS = 1e-05
+CHUNKS = 4
+SEQS, DPS = 8, 4
 SCALE = HEAD_DIM ** (-0.5)
 NT = (((1,), (1,)), ((), ()))
 TN = (((0,), (0,)), ((), ()))
@@ -67,7 +69,7 @@
     gm = dot(cot_ref[...], w_ref[...], NT)
     dgate_ref[...] = (gm * normed * gain).astype(jnp.bfloat16)
     scaled = gm * gate
-    part = jnp.sum(scaled * normed, axis=0, keepdims=True)
+    part = jnp.sum((scaled * normed).reshape(BLK // 8, 8, -1), axis=0)
 
     @pl.when(i == 0)
     def _():
@@ -145,15 +147,16 @@
         kv += [k_all, v_all]
     whole = pl.BlockSpec((width, width), lambda i, far, tr, my: (0, 0))
     vec = pl.BlockSpec((1, width), lambda i, far, tr, my: (0, 0))
+    vec8 = pl.BlockSpec((8, width), lambda i, far, tr, my: (0, 0))
     big = jax.ShapeDtypeStruct((rows, width), jnp.bfloat16)
     return pl.pallas_call(
         functools.partial(query_kernel, nb),
-        out_shape=(big, big, big, big, big, jax.ShapeDtypeStruct((1, width), jnp.float32)),
+        out_shape=(big, big, big, big, big, jax.ShapeDtypeStruct((8, width), jnp.float32)),
         grid_spec=pltpu.PrefetchScalarGridSpec(
             num_scalar_prefetch=3,
             grid=(nb,),
             in_specs=[own] + kv_specs + [own, own, vec, whole],
-            out_specs=(own, own, own, own, own, vec),
+            out_specs=(own, own, own, own, own, vec8),
             scratch_shapes=[
                 pltpu.VMEM((BLK, width), jnp.float32),
                 pltpu.VMEM((HEADS, BLK, (2 + FAR) * BLK), jnp.float32),
@@ -216,6 +219,238 @@
     return qi.astype(jnp.int32), ki.astype(jnp.int32), on.astype(jnp.int32)
 
 
+def places():
+    me = lax.axis_index("seq")
+    x, y = (me // 2) % 2, (me // 4) % 2
+    side = me + 1 - 2 * (me % 2)
+    over_x = 2 - 4 * x
+    over_y = 4 - 8 * y
+    return me, side, me + over_x, me + over_y, me + over_x + over_y
+
+
+def greet(peers):
+    barrier = pltpu.get_barrier_semaphore()
+    for peer in peers:
+        pl.semaphore_signal(barrier, inc=1, device_id=peer, device_id_type=pl.DeviceIdType.MESH)
+    pl.semaphore_wait(barrier, len(peers))
+
+
+class Spread:
+    def __init__(self, src, dst, send, recv, own):
+        self.src, self.dst, self.send, self.recv, self.own = src, dst, send, recv, own
+        self.me, self.side, self.px, self.py, self.pd = places()
+        self.rows = src.shape[0]
+        self.step = self.rows // CHUNKS
+        self.sent = []
+
+    def slot(self, origin, j):
+        return self.dst.at[pl.ds(pl.multiple_of(origin * self.rows, self.rows) + j * self.step, self.step)]
+
+    def copy(self, src, origin, kind, j, to):
+        return pltpu.make_async_remote_copy(
+            src_ref=src,
+            dst_ref=self.slot(origin, j),
+            send_sem=self.send.at[kind, j],
+            recv_sem=self.recv.at[kind, j],
+            device_id={"seq": to},
+            device_id_type=pl.DeviceIdType.MESH,
+        )
+
+    def push(self, src, origin, kind, j, to):
+        made = self.copy(src, origin, kind, j, to)
+        made.start()
+        self.sent.append(made)
+
+    def take(self, origin, kind, j):
+        self.copy(self.slot(origin, j), origin, kind, j, self.side).wait_recv()
+
+    def begin(self):
+        self.keep = pltpu.make_async_copy(
+            self.src,
+            self.dst.at[pl.ds(pl.multiple_of(self.me * self.rows, self.rows), self.rows)],
+            self.own,
+        )
+        half = CHUNKS // 2
+        for n in range(CHUNKS):
+            j, i = n, (n + half) % CHUNKS
+            self.push(self.src.at[pl.ds(j * self.step, self.step)], self.me, 0, j, self.px)
+            self.push(self.src.at[pl.ds(i * self.step, self.step)], self.me, 1, i, self.py)
+        for j in range(CHUNKS):
+            self.push(self.src.at[pl.ds(j * self.step, self.step)], self.me, 3, j, self.side)
+        self.keep.start()
+
+    def relay(self):
+        half = CHUNKS // 2
+        for n in range(CHUNKS):
+            j, i = n, (n + half) % CHUNKS
+            self.take(self.px, 0, j)
+            if n < half:
+                self.push(self.slot(self.px, j), self.px, 2, j, self.py)
+            self.push(self.slot(self.px, j), self.px, 4, j, self.side)
+            self.take(self.py, 1, i)
+            if n < half:
+                self.push(self.slot(self.py, i), self.py, 2, i, self.px)
+            self.push(self.slot(self.py, i), self.py, 5, i, self.side)
+
+    def finish(self):
+        half = CHUNKS // 2
+        for n in range(half):
+            for j in (n, n + half):
+                self.take(self.pd, 2, j)
+                self.push(self.slot(self.pd, j), self.pd, 6, j, self.side)
+
+    def drain(self):
+        far = self.side - self.me
+        for kind, origin in ((3, self.me), (4, self.px), (5, self.py), (6, self.pd)):
+            for j in range(CHUNKS):
+                self.take(origin + far, kind, j)
+        for made in self.sent:
+            made.wait_send()
+        self.keep.wait()
+
+
+def seq_peers():
+    _, side, px, py, pd = places()
+    return [{"seq": p} for p in (side, px, py, pd)]
+
+
+def spread_kernel(count, *refs):
+    srcs, dsts = refs[:count], refs[count : 2 * count]
+    send, recv, own = refs[2 * count :]
+    greet(seq_peers())
+    jobs = [
+        Spread(srcs[a], dsts[a], send.at[a], recv.at[a], own.at[a]) for a in range(count)
+    ]
+    for job in jobs:
+        job.begin()
+    for job in jobs:
+        job.relay()
+    for job in jobs:
+        job.finish()
+    for job in jobs:
+        job.drain()
+
+
+def spread(arrays, ident):
+    count = len(arrays)
+    rows, width = arrays[0].shape
+    anywhere = pl.BlockSpec(memory_space=pl.ANY)
+    full = jax.ShapeDtypeStruct((SEQS * rows, width), jnp.bfloat16)
+    return pl.pallas_call(
+        functools.partial(spread_kernel, count),
+        out_shape=(full,) * count,
+        in_specs=[anywhere] * count,
+        out_specs=(anywhere,) * count,
+        scratch_shapes=[
+            pltpu.SemaphoreType.DMA((count, 7, CHUNKS)),
+            pltpu.SemaphoreType.DMA((count, 7, CHUNKS)),
+            pltpu.SemaphoreType.DMA((count,)),
+        ],
+        compiler_params=pltpu.CompilerParams(collective_id=ident, has_side_effects=True),
+        name="spread_rows",
+    )(*arrays)
+
+
+def tail_kernel(
+    c_ref, gw_ref, dg_ref, c_all, gw_out, dg_out,
+    got_side, mid, got_z, low, got_xy, dg_side, dg_z, dg_yx,
+    send, recv, own, red_send, red_recv,
+):
+    greet(seq_peers() + [{"dp": lax.rem(lax.axis_index("dp") + k, DPS)} for k in range(1, DPS)])
+    me, side, px, py, pd = places()
+    core = me % 2
+    z = lax.axis_index("dp")
+    yx = me // 2
+    job = Spread(c_ref, c_all, send, recv, own)
+    sent = []
+
+    def push(src, dst, at, to):
+        made = pltpu.make_async_remote_copy(
+            src_ref=src, dst_ref=dst, send_sem=red_send.at[at], recv_sem=red_recv.at[at],
+            device_id=to, device_id_type=pl.DeviceIdType.MESH,
+        )
+        made.start()
+        sent.append(made)
+        return made
+
+    one = push(gw_ref.at[1 - core], got_side, 0, {"seq": side})
+    dg_one = push(dg_ref, dg_side, 1, {"seq": side})
+    job.begin()
+    one.wait_recv()
+    dg_one.wait_recv()
+    for p in range(DPS):
+        mid[p] = (
+            gw_ref[core, p].astype(jnp.float32) + got_side[p].astype(jnp.float32)
+        ).astype(jnp.bfloat16)
+    dg_z[z] = dg_ref[...] + dg_side[...]
+    twos = []
+    for k in range(1, DPS):
+        to = lax.rem(z + k, DPS)
+        twos.append(push(mid.at[to], got_z.at[k - 1], 2 * k, {"dp": to}))
+        twos.append(push(dg_z.at[z], dg_z.at[z], 2 * k + 1, {"dp": to}))
+    job.relay()
+    for two in twos:
+        two.wait_recv()
+    total = gw_ref[core, z].astype(jnp.float32) + got_side[z].astype(jnp.float32)
+    for k in range(DPS - 1):
+        total += got_z[k].astype(jnp.float32)
+    low[...] = total.astype(jnp.bfloat16).reshape(low.shape)
+    dg_yx[yx] = dg_z[0] + dg_z[1] + dg_z[2] + dg_z[3]
+    threes = []
+    for k, to in enumerate((px, py, pd)):
+        threes.append(push(low.at[to // 2], got_xy.at[k], 8 + 2 * k, {"seq": to}))
+        threes.append(push(dg_yx.at[yx], dg_yx.at[yx], 9 + 2 * k, {"seq": to}))
+    job.finish()
+    for three in threes:
+        three.wait_recv()
+    result = low[yx].astype(jnp.float32)
+    for k in range(3):
+        result += got_xy[k].astype(jnp.float32)
+    gw_out[...] = result
+    dg_out[...] = dg_yx[0] + dg_yx[1] + dg_yx[2] + dg_yx[3]
+    job.drain()
+    for made in sent:
+        made.wait_send()
+
+
+def tail(c, gw, dg):
+    rows, width = c.shape
+    depth = width // (SEQS * DPS)
+    anywhere = pl.BlockSpec(memory_space=pl.ANY)
+    vmem = pl.BlockSpec(memory_space=pltpu.VMEM)
+    part = (SEQS // 2) * depth
+    b16 = jnp.bfloat16
+    return pl.pallas_call(
+        tail_kernel,
+        out_shape=(
+            jax.ShapeDtypeStruct((SEQS * rows, width), b16),
+            jax.ShapeDtypeStruct((depth, width), jnp.float32),
+            jax.ShapeDtypeStruct(dg.shape, jnp.float32),
+        ),
+        in_specs=[anywhere, vmem, vmem],
+        out_specs=(anywhere, vmem, vmem),
+        scratch_shapes=[
+            pltpu.VMEM((DPS, part, width), b16),
+            pltpu.VMEM((DPS, part, width), b16),
+            pltpu.VMEM((DPS - 1, part, width), b16),
+            pltpu.VMEM((SEQS // 2, depth, width), b16),
+            pltpu.VMEM((3, depth, width), b16),
+            pltpu.VMEM(dg.shape, jnp.float32),
+            pltpu.VMEM((DPS,) + dg.shape, jnp.float32),
+            pltpu.VMEM((SEQS // 2,) + dg.shape, jnp.float32),
+            pltpu.SemaphoreType.DMA((7, CHUNKS)),
+            pltpu.SemaphoreType.DMA((7, CHUNKS)),
+            pltpu.SemaphoreType.DMA,
+            pltpu.SemaphoreType.DMA((14,)),
+            pltpu.SemaphoreType.DMA((14,)),
+        ],
+        compiler_params=pltpu.CompilerParams(
+            collective_id=2, has_side_effects=True, vmem_limit_bytes=40 * 2**20
+        ),
+        name="tail_exchange",
+    )(c, gw, dg)
+
+
 def gather(rows):
     return lax.all_gather(rows, "seq", axis=0, tiled=True)
 
@@ -227,18 +462,27 @@
     me = lax.axis_index("seq").astype(jnp.int32)
     far = far_blocks[0].reshape(-1)
     flags = treated[0]
-    k_all, v_all = gather(k), gather(v)
-    q_all = gather(q)
+    seqs, dps = lax.axis_size("seq"), lax.axis_size("dp")
+    direct = (seqs, dps) == (SEQS, DPS)
+    if direct:
+        k_all, v_all = spread([k, v], 1)
+        q_late, k_all, v_all = lax.optimization_barrier((q, k_all, v_all))
+        q_all = gather(q_late)
+    else:
+        k_all, v_all, q_all = gather(k), gather(v), gather(q)
     out, dq, dgate, mixed, c, dgain = run_query(
         q, k, v, k_all, v_all, gate, cot, far, flags, me[None], gain[None], w
     )
-    c_all = gather(c)
     grad_weight = dot(mixed, cot, TN)
-    seqs, dps = lax.axis_size("seq"), lax.axis_size("dp")
-    grad_weight = grad_weight.reshape(seqs, dps, -1, width)
-    grad_weight = lax.psum_scatter(grad_weight, "dp", scatter_dimension=1, tiled=False)
-    grad_weight = lax.psum_scatter(grad_weight, "seq", scatter_dimension=0, tiled=False)
-    dgain = lax.psum(dgain[0], ("seq", "dp"))
+    if direct:
+        parts = grad_weight.astype(jnp.bfloat16).reshape(seqs // 2, 2, dps, -1, width)
+        parts = parts.transpose(1, 2, 0, 3, 4).reshape(2, dps, -1, width)
+        c_all, grad_weight, dgain = tail(c, parts, dgain)
+        dgain = jnp.sum(dgain, axis=0)
+    else:
+        c_all = gather(c)
+        grad_weight = lax.psum_scatter(grad_weight, ("seq", "dp"), scatter_dimension=0, tiled=True)
+        dgain = lax.psum(jnp.sum(dgain, axis=0), ("seq", "dp"))
     qi, ki, on = key_plan(far, flags, me, nb)
     dk, dv = run_keys(qi, ki, on, q_all, c_all, k, v)
     return out[None], dq[None], dk[None], dv[None], dgate[None], grad_weight, dgain

time: 483 us -> 230 us (0.48)
  waiting for transfers between devices: 339 us -> 0.02 us
  Pallas kernels: 67.9 us -> 194 us
  blocking collectives: 39.7 us -> 0 us
    all_gather x4 -> x1, waiting for transfers between devices: 184 us -> 0.01 us  [gather(): return lax.all_gather(rows, 'seq', axis=0, tiled=True)]
    unnamed x7 -> x1, waiting for transfers between devices: 156 us -> 0.02 us
    pallas_call x0 -> x2, Pallas kernels: none -> 127 us  [the longest x1 75.5 us: spread(): pl.pallas_call(functools.partial(spread_kernel, count), out_shape=(full,)...]
    psum x1 -> x0, blocking collectives: 39.7 us -> none  [body(): dgain = lax.psum(dgain[0], ('seq', 'dp'))]
  transfers between devices with their start and end apart: 6 -> 1, of which waited for: 5 -> 0; matrix products, arithmetic and copies ran while one was open for 1% -> 2% of each run, Pallas kernels for 8% -> 35%
where the time goes in v2:
time: 230 us
  Pallas kernels  194 us (84%)
  local copies, waits for them, and re-layouts  18.9 us (8%)
  between operations  14.2 us (6%)
    pallas_call x1, Pallas kernels, spread(): pl.pallas_call(functools.partial(spread_kernel, count), out_shape=(full,)...  75.5 us
    pallas_call x1, Pallas kernels, tail(): pl.pallas_call(tail_kernel, out_shape=(jax.ShapeDtypeStruct((SEQS * rows,...  51.5 us
    pallas_call x1, Pallas kernels, run_keys(): pl.pallas_call(functools.partial(key_kernel, steps), out_shape=(big, big)...  39.1 us
    pallas_call x1, Pallas kernels, run_query(): pl.pallas_call(functools.partial(query_kernel, nb), out_shape=(big, big,...  28.1 us
    unnamed x30, local copies, waits for them, and re-layouts  17.2 us
  transfers between devices with their start and end apart: 1, of which 0 were waited for; matrix products, arithmetic and copies ran while one was open for 2% of the time, Pallas kernels for 35%

profile of v2, /device:TPU:0, one launch (start us, length us, event | category | flops | bytes accessed | tf_op | source)
XLA Modules:
  0.0 229.8 jit_solution(9600772247695179783)
XLA Ops:
  7.2 75.5 %spread_rows.1 = (bf16[4096,1024]{1,0:T(8,128)(2,1)}, bf16[4096,1024]{1,0:T(8,128)(2,1)}) custom-call(bf16[512,1024]{1,0:T(8,128)(2,1)} %bitcast.20, bf16[512,1024]{1,0:T(8,128)(2,1)} %bitcast.23), custom_call_target="tpu_custom_call" | custom-call | tf_op jit(solution)/shard_map/spread_rows/pallas_call | solution.py:339
  82.8 0.8 copy.20
  83.6 0.1 reshape_squeeze.3.far_s
  83.7 1.2 copy-done
  84.9 1.2 copy-done.2
  86.1 1.2 copy-done.7
  87.4 1.2 copy-done.9
  88.6 1.3 copy-done.10
  89.9 0.7 copy-done.11
  90.6 0.7 copy-done.12
  91.3 28.1 %query_side.1 = (bf16[512,1024]{1,0:T(8,128)(2,1)}, bf16[512,1024]{1,0:T(8,128)(2,1)}, bf16[512,1024]{1,0:T(8,128)(2,1)}, bf16[512,1024]{1,0:T(8,128)(2,1)S(1)},...) custom-call(s32[128]{0:T(128)S(1)} %reshape_squeeze.3.far_s, s32[32]{0:T(128)S(1)} %bitcast.32, s32[1]{0:T(128)} %bitcast.1.my_s, ...), custom_call_target="tpu_custom_call" | custom-call | flops 8000000000 | bytes 25165824 | tf_op jit(solution)/shard_map/query_side/pallas_call | solution.py:152
  119.4 1.3 convolution_convert_fusion
  120.7 1.6 copy.21
  122.3 1.6 copy-done.6
  123.9 51.5 %tail_exchange.1 = (bf16[4096,1024]{1,0:T(8,128)(2,1)S(1)}, f32[32,1024]{1,0:T(8,128)S(1)}, f32[8,1024]{1,0:T(8,128)S(1)}) custom-call(bf16[512,1024]{1,0:T(8,128)(2,1)S(1)} %get-tuple-element.30.c_ref, bf16[2,4,128,1024]{3,2,1,0:T(8,128)(2,1)S(1)} %bitcast.26, f32[8,1024]{1,0:T(8,128)S(1)} %get-tuple-element.32.dg_ref), custom_call_target="tpu_custom_call" | custom-call | tf_op jit(solution)/shard_map/tail_exchange/pallas_call | solution.py:423
  175.4 3.2 %copy-done.5 = bf16[4096,1024]{1,0:T(8,128)(2,1)} copy-done((bf16[4096,1024]{1,0:T(8,128)(2,1)}, bf16[4096,1024]{1,0:T(8,128)(2,1)S(1)}, u32[]{:S(2)}) %copy-start.5) | copy-done | bytes 8388632
  178.6 0.6 reduce_sum.59
  179.3 0.1 convert_reduce_fusion
  179.4 0.1 select_reduce_fusion
  179.5 0.1 select_reduce_fusion.1
  179.7 0.1 pad_add_fusion
  179.8 3.4 %copy-done.4 = bf16[4096,1024]{1,0:T(8,128)(2,1)S(1)} copy-done((bf16[4096,1024]{1,0:T(8,128)(2,1)S(1)}, bf16[4096,1024]{1,0:T(8,128)(2,1)}, u32[]{:S(2)}) %copy-start.4) | copy-done | bytes 8388632
  183.2 39.1 %key_side.1 = (bf16[512,1024]{1,0:T(8,128)(2,1)}, bf16[512,1024]{1,0:T(8,128)(2,1)}) custom-call(s32[24]{0:T(128)S(1)} %get-tuple-element.42.qi_s, s32[24]{0:T(128)S(1)} %get-tuple-element.43.ki_s, s32[24]{0:T(128)S(1)} %pad_add_fusion.2.on_s, bf16[4096,1024]{1,0:T(8,128)(2,1)S(1)} %copy-done.4, bf16[4096,1024]{1,0:T(8,128)(2,1)} %copy-done.5, ...), custom_call_target="tpu_custom_call" | custom-call | flops 4000000000 | bytes 16777216 | tf_op jit(solution)/shard_map/key_side/pallas_call | solution.py:179
  222.3 0.7 copy.23
  (30 shorter events, 0.2 us)
Async XLA Ops:
  7.2 76.5 %copy-start.8 = (bf16[1024,1024]{1,0:T(8,128)(2,1)S(1)}, bf16[1024,1024]{1,0:T(8,128)(2,1)}, u32[]{:S(2)}) copy-start(bf16[1024,1024]{1,0:T(8,128)(2,1)} %w_ref.1) | copy-start | bytes 6291460
  7.2 172.6 %all-gather.2.cloned.1.call-start = ((), (), s32[]{:S(2)}) async-start(), calls=%async_computation | async-start | bytes 9437184 | tf_op jit(solution)/shard_map/all_gather | solution.py:455
  83.7 1.2 copy-start
  84.9 1.2 copy-start.2
  86.1 1.2 copy-start.7
  87.4 1.2 copy-start.9
  88.6 1.3 copy-start.10
  89.9 0.7 copy-start.11
  90.6 0.7 copy-start.12
  120.6 58.7 %copy-start.13 = (s32[1,32]{1,0:T(1,128)S(1)}, s32[1,32]{1,0:T(1,128)}, u32[]{:S(2)}) copy-start(s32[1,32]{1,0:T(1,128)} %param.15) | copy-start | bytes 388
  120.7 59.2 %copy-start.1 = (bf16[1,512,1024]{2,1,0:T(8,128)(2,1)S(1)}, bf16[1,512,1024]{2,1,0:T(8,128)(2,1)}, u32[]{:S(2)}) copy-start(bf16[1,512,1024]{2,1,0:T(8,128)(2,1)} %param.10) | copy-start | bytes 3145732
  120.7 59.2 %copy-start.3 = (bf16[1,512,1024]{2,1,0:T(8,128)(2,1)S(1)}, bf16[1,512,1024]{2,1,0:T(8,128)(2,1)}, u32[]{:S(2)}) copy-start(bf16[1,512,1024]{2,1,0:T(8,128)(2,1)} %param.11) | copy-start | bytes 3145732
  122.2 1.6 copy-start.6
  175.4 3.2 %copy-start.5 = (bf16[4096,1024]{1,0:T(8,128)(2,1)}, bf16[4096,1024]{1,0:T(8,128)(2,1)S(1)}, u32[]{:S(2)}) copy-start(bf16[4096,1024]{1,0:T(8,128)(2,1)S(1)} %get-tuple-element.33.c_ref) | copy-start | bytes 25165828
  179.8 3.4 %copy-start.4 = (bf16[4096,1024]{1,0:T(8,128)(2,1)S(1)}, bf16[4096,1024]{1,0:T(8,128)(2,1)}, u32[]{:S(2)}) copy-start(bf16[4096,1024]{1,0:T(8,128)(2,1)} %all-gather.2.cloned.1.call-done.q_ref) | copy-start | bytes 25165828
Sparse Core Ops, SparseCore 0:
  82.9 60.5 all-gather.1

commit v3 on v2

--- a/solution.py
+++ b/solution.py
@@ -34,29 +34,27 @@
 def query_kernel(
     nb, far_s, treated_s, my_s, q_ref, k0, v0, k1, v1, k2, v2, k3, v3, k4, v4, k5, v5,
     gate_ref, cot_ref, gain_ref, w_ref,
-    out_ref, dq_ref, dgate_ref, mixed_ref, c_ref, dgain_ref, att, slope,
+    out_ref, dq_ref, dgate_ref, mixed_ref, c_ref, dgain_ref, att, slope, vals, keys,
 ):
     i = pl.program_id(0)
     block = my_s[0] * nb + i
-    keys = (k0, k1, k2, k3, k4, k5)
-    vals = (v0, v1, v2, v3, v4, v5)
     flags = [None, (block > 0).astype(jnp.float32)]
     flags += [treated_s[far_s[block * FAR + f]].astype(jnp.float32) for f in range(FAR)]
+    for p, (one_k, one_v) in enumerate(zip((k0, k1, k2, k3, k4, k5), (v0, v1, v2, v3, v4, v5))):
+        at = slice(p * BLK, (p + 1) * BLK)
+        keys[at] = one_k[...]
+        vals[at] = one_v[...] if p == 0 else one_v[...] * flags[p].astype(jnp.bfloat16)
     row = lax.broadcasted_iota(jnp.int32, (BLK, BLK), 0)
     col = lax.broadcasted_iota(jnp.int32, (BLK, BLK), 1)
     tril = (row >= col).astype(jnp.float32)
     for h in range(HEADS):
         hs = slice(h * HEAD_DIM, (h + 1) * HEAD_DIM)
         q = q_ref[:, hs]
-        acts = []
-        for p in range(2 + FAR):
-            act, der = silu_parts(dot(q, keys[p][:, hs], NT))
-            m = tril if p == 0 else flags[p]
-            acts.append((act * m).astype(jnp.bfloat16))
-            slope[h, :, p * BLK : (p + 1) * BLK] = der * m
-        att[:, hs] = dot(
-            jnp.concatenate(acts, axis=1), jnp.concatenate([v[:, hs] for v in vals], axis=0)
-        )
+        act, der = silu_parts(dot(q, keys[:, hs], NT))
+        act = jnp.concatenate([act[:, :BLK] * tril, act[:, BLK:]], axis=1)
+        slope[h, :, :BLK] = der[:, :BLK] * tril
+        slope[h, :, BLK:] = der[:, BLK:]
+        att[:, hs] = dot(act.astype(jnp.bfloat16), vals[:, hs])
     attention = att[...]
     centered = attention - jnp.mean(attention, axis=1, keepdims=True)
     inv_std = lax.rsqrt(jnp.mean(centered * centered, axis=1, keepdims=True) + EPS)
@@ -88,41 +86,43 @@
     for h in range(HEADS):
         hs = slice(h * HEAD_DIM, (h + 1) * HEAD_DIM)
         ch = c_ref[:, hs]
-        ds = []
-        for p in range(2 + FAR):
-            da = dot(ch, vals[p][:, hs], NT)
-            ds.append((da * slope[h, :, p * BLK : (p + 1) * BLK]).astype(jnp.bfloat16))
-        dq = dot(
-            jnp.concatenate(ds, axis=1), jnp.concatenate([k[:, hs] for k in keys], axis=0)
-        )
+        ds = dot(ch, vals[:, hs], NT) * slope[h]
+        dq = dot(ds.astype(jnp.bfloat16), keys[:, hs])
         dq_ref[:, hs] = (dq * SCALE).astype(jnp.bfloat16)
 
 
-def key_kernel(
-    steps, qi_s, ki_s, on_s, q_ref, c_ref, k_ref, v_ref, dk_ref, dv_ref, dk_acc, dv_acc
-):
+def key_kernel(nb, steps, qi_s, ki_s, on_s, *refs):
+    q_refs, c_refs = refs[:nb], refs[nb : 2 * nb]
+    k_ref, v_ref, dk_ref, dv_ref, dk_acc, dv_acc = refs[2 * nb :]
     r = pl.program_id(0)
+    row = lax.broadcasted_iota(jnp.int32, (BLK, BLK), 0)
+    col = lax.broadcasted_iota(jnp.int32, (BLK, BLK), 1)
+    upper = (col >= row).astype(jnp.float32)
 
     @pl.when(r == 0)
     def _():
-        dk_acc[...] = jnp.zeros_like(dk_acc)
-        dv_acc[...] = jnp.zeros_like(dv_acc)
-
-    at = pl.ds(pl.multiple_of(ki_s[r] * BLK, BLK), BLK)
-    mode = on_s[r]
-    on = (mode > 0).astype(jnp.float32)
-    off_diag = jnp.where(mode == 2, 0.0, on)
-    row = lax.broadcasted_iota(jnp.int32, (BLK, BLK), 0)
-    col = lax.broadcasted_iota(jnp.int32, (BLK, BLK), 1)
-    m = jnp.where(col >= row, on, off_diag)
-    for h in range(HEADS):
-        hs = slice(h * HEAD_DIM, (h + 1) * HEAD_DIM)
-        q = q_ref[:, hs]
-        c = c_ref[:, hs]
-        act, der = silu_parts(dot(k_ref[at, hs], q, NT))
-        da = dot(v_ref[at, hs], c, NT)
-        dv_acc[at, hs] += dot((act * m).astype(jnp.bfloat16), c)
-        dk_acc[at, hs] += dot((da * der * m).astype(jnp.bfloat16), q)
+        for n in range(nb):
+            at = slice(n * BLK, (n + 1) * BLK)
+            for h in range(HEADS):
+                hs = slice(h * HEAD_DIM, (h + 1) * HEAD_DIM)
+                q, c = q_refs[n][:, hs], c_refs[n][:, hs]
+                act, der = silu_parts(dot(k_ref[at, hs], q, NT))
+                da = dot(v_ref[at, hs], c, NT)
+                dv_acc[at, hs] = dot((act * upper).astype(jnp.bfloat16), c)
+                dk_acc[at, hs] = dot((da * der * upper).astype(jnp.bfloat16), q)
+
+    @pl.when(r > 0)
+    def _():
+        for n in range(nb):
+            at = pl.ds(pl.multiple_of(ki_s[r * nb + n] * BLK, BLK), BLK)
+            on = (on_s[r * nb + n] > 0).astype(jnp.bfloat16)
+            for h in range(HEADS):
+                hs = slice(h * HEAD_DIM, (h + 1) * HEAD_DIM)
+                q, c = q_refs[n][:, hs], c_refs[n][:, hs] * on
+                act, der = silu_parts(dot(k_ref[at, hs], q, NT))
+                da = dot(v_ref[at, hs], c, NT)
+                dv_acc[at, hs] += dot(act.astype(jnp.bfloat16), c)
+                dk_acc[at, hs] += dot((da * der).astype(jnp.bfloat16), q)
 
     @pl.when(r == steps - 1)
     def _():
@@ -160,9 +160,11 @@
             scratch_shapes=[
                 pltpu.VMEM((BLK, width), jnp.float32),
                 pltpu.VMEM((HEADS, BLK, (2 + FAR) * BLK), jnp.float32),
+                pltpu.VMEM(((2 + FAR) * BLK, width), jnp.bfloat16),
+                pltpu.VMEM(((2 + FAR) * BLK, width), jnp.bfloat16),
             ],
         ),
-        compiler_params=pltpu.CompilerParams(vmem_limit_bytes=40 * 2**20),
+        compiler_params=pltpu.CompilerParams(vmem_limit_bytes=60 * 2**20),
         cost_estimate=pl.CostEstimate(
             flops=8 * 10**9, bytes_accessed=24 * 2**20, transcendentals=3 * 10**6
         ),
@@ -172,26 +174,31 @@
 
 def run_keys(qi, ki, on, q_all, c_all, k, v):
     rows, width = k.shape
-    steps = qi.shape[0]
-    pick = pl.BlockSpec((BLK, width), lambda r, qi, ki, on: (qi[r], 0))
+    nb = rows // BLK
+    steps = qi.shape[0] // nb
+
+    def pick(n):
+        return pl.BlockSpec((BLK, width), lambda r, qi, ki, on: (qi[r * nb + n], 0))
+
+    picks = [pick(n) for n in range(nb)]
     whole = pl.BlockSpec((rows, width), lambda r, qi, ki, on: (0, 0))
     big = jax.ShapeDtypeStruct((rows, width), jnp.bfloat16)
     return pl.pallas_call(
-        functools.partial(key_kernel, steps),
+        functools.partial(key_kernel, nb, steps),
         out_shape=(big, big),
         grid_spec=pltpu.PrefetchScalarGridSpec(
             num_scalar_prefetch=3,
             grid=(steps,),
-            in_specs=[pick, pick, whole, whole],
+            in_specs=picks + picks + [whole, whole],
             out_specs=(whole, whole),
             scratch_shapes=[pltpu.VMEM((rows, width), jnp.float32)] * 2,
         ),
-        compiler_params=pltpu.CompilerParams(vmem_limit_bytes=40 * 2**20),
+        compiler_params=pltpu.CompilerParams(vmem_limit_bytes=60 * 2**20),
         cost_estimate=pl.CostEstimate(
             flops=4 * 10**9, bytes_accessed=16 * 2**20, transcendentals=3 * 10**6
         ),
         name="key_side",
-    )(qi, ki, on, q_all, c_all, k, v)
+    )(qi, ki, on, *[q_all] * nb, *[c_all] * nb, k, v)
 
 
 def key_plan(far, treated, me, nb):
@@ -346,7 +353,7 @@
             pltpu.SemaphoreType.DMA((count, 7, CHUNKS)),
             pltpu.SemaphoreType.DMA((count,)),
         ],
-        compiler_params=pltpu.CompilerParams(collective_id=ident, has_side_effects=True),
+        compiler_params=pltpu.CompilerParams(collective_id=ident, has_side_effects=True, vmem_limit_bytes=60 * 2**20),
         name="spread_rows",
     )(*arrays)
 
@@ -445,7 +452,7 @@
             pltpu.SemaphoreType.DMA((14,)),
         ],
         compiler_params=pltpu.CompilerParams(
-            collective_id=2, has_side_effects=True, vmem_limit_bytes=40 * 2**20
+            collective_id=2, has_side_effects=True, vmem_limit_bytes=60 * 2**20
         ),
         name="tail_exchange",
     )(c, gw, dg)

time: 230 us -> 226 us (0.983)
  local copies, waits for them, and re-layouts: 18.9 us -> 3.6 us
  Pallas kernels: 194 us -> 202 us
    unnamed x30 -> x10, local copies, waits for them, and re-layouts: 17.2 us -> 1.44 us
    pallas_call x1, Pallas kernels: 51.5 us -> 60.5 us  [tail(): pl.pallas_call(tail_kernel, out_shape=(jax.ShapeDtypeStruct((SEQS * rows,...]
  transfers between devices with their start and end apart: 1 -> 1, of which waited for: 0 -> 0; matrix products, arithmetic and copies ran while one was open for 2% -> 4% of each run, Pallas kernels for 35% -> 39%
where the time goes in v3:
time: 226 us
  Pallas kernels  202 us (89%)
  between operations  14.1 us (6%)
  local copies, waits for them, and re-layouts  3.6 us (2%)
  other arithmetic  3 us (1%)
  matrix products  2.83 us (1%)
    pallas_call x1, Pallas kernels, spread(): pl.pallas_call(functools.partial(spread_kernel, count), out_shape=(full,)...  75.5 us
    pallas_call x1, Pallas kernels, tail(): pl.pallas_call(tail_kernel, out_shape=(jax.ShapeDtypeStruct((SEQS * rows,...  60.5 us
    pallas_call x1, Pallas kernels, run_keys(): pl.pallas_call(functools.partial(key_kernel, nb, steps), out_shape=(big,...  39.1 us
    pallas_call x1, Pallas kernels, run_query(): pl.pallas_call(functools.partial(query_kernel, nb), out_shape=(big, big,...  26.9 us
  transfers between devices with their start and end apart: 1, of which 0 were waited for; matrix products, arithmetic and copies ran while one was open for 4% of the time, Pallas kernels for 39%

profile of v3, /device:TPU:0, one launch (start us, length us, event | category | flops | bytes accessed | tf_op | source)
XLA Modules:
  0.0 225.8 jit_solution(14626532030302892764)
XLA Ops:
  7.2 0.0 all-gather.2.cloned.1.call-start
  7.2 75.5 %spread_rows.1 = (bf16[4096,1024]{1,0:T(8,128)(2,1)}, bf16[4096,1024]{1,0:T(8,128)(2,1)}) custom-call(bf16[512,1024]{1,0:T(8,128)(2,1)} %bitcast.20, bf16[512,1024]{1,0:T(8,128)(2,1)} %bitcast.23), custom_call_target="tpu_custom_call" | custom-call | tf_op jit(solution)/shard_map/spread_rows/pallas_call | solution.py:346
  82.8 0.0 all-gather.2.cloned.1.call-update
  82.8 0.8 copy.20
  83.6 0.6 reshape_squeeze.3.far_s
  84.2 0.0 copy-start
  84.2 26.9 %query_side.1 = (bf16[512,1024]{1,0:T(8,128)(2,1)}, bf16[512,1024]{1,0:T(8,128)(2,1)}, bf16[512,1024]{1,0:T(8,128)(2,1)}, bf16[512,1024]{1,0:T(8,128)(2,1)}, bf1...) custom-call(s32[128]{0:T(128)} %reshape_squeeze.3.far_s, s32[32]{0:T(128)} %bitcast.33, s32[1]{0:T(128)} %bitcast.1.my_s, ...), custom_call_target="tpu_custom_call" | custom-call | flops 8000000000 | bytes 25165824 | tf_op jit(solution)/shard_map/query_side/pallas_call | solution.py:152
  111.1 0.0 copy-done
  111.1 2.8 %convolution_convert_fusion = bf16[1024,1024]{1,0:T(8,128)(2,1)S(1)} fusion(bf16[512,1024]{1,0:T(8,128)(2,1)} %get-tuple-element.31, bf16[1,512,1024]{2,1,0:T(8,128)(2,1)S(1)} %copy-done), kind=kOutput, calls=%fused_computation | convolution fusion | flops 1074790400 | bytes 4194304 | tf_op jit(solution)/shard_map/dot_general | solution.py:23
  114.0 0.0 copy-start.2
  114.0 0.0 copy-start.3
  114.0 1.5 copy.21
  115.5 60.5 %tail_exchange.1 = (bf16[4096,1024]{1,0:T(8,128)(2,1)}, f32[32,1024]{1,0:T(8,128)}, f32[8,1024]{1,0:T(8,128)}) custom-call(bf16[512,1024]{1,0:T(8,128)(2,1)} %get-tuple-element.30.c_ref, bf16[2,4,128,1024]{3,2,1,0:T(8,128)(2,1)} %bitcast.26, f32[8,1024]{1,0:T(8,128)} %get-tuple-element.32.dg_ref), custom_call_target="tpu_custom_call" | custom-call | tf_op jit(solution)/shard_map/tail_exchange/pallas_call | solution.py:430
  176.1 1.4 reduce_sum.59
  177.5 0.0 copy-done.2
  177.5 0.1 convert_reduce_fusion
  177.6 0.0 copy-done.3
  177.6 0.1 select_reduce_fusion
  177.7 0.1 select_reduce_fusion.1
  177.9 0.7 pad_add_fusion.2.on_s
  178.5 0.6 pad_add_fusion
  179.1 39.1 %key_side.1 = (bf16[512,1024]{1,0:T(8,128)(2,1)}, bf16[512,1024]{1,0:T(8,128)(2,1)}) custom-call(s32[24]{0:T(128)} %get-tuple-element.42.qi_s, s32[24]{0:T(128)} %get-tuple-element.43.ki_s, s32[24]{0:T(128)} %pad_add_fusion.2.on_s, bf16[4096,1024]{1,0:T(8,128)(2,1)} %all-gather.2.cloned.1.call-done.refs_0_.refs_1_.refs_2_.refs_3_, ...), custom_call_target="tpu_custom_call" | custom-call | flops 4000000000 | bytes 16777216 | tf_op jit(solution)/shard_map/key_side/pallas_call | solution.py:186
  218.3 0.0 copy-done.1
  218.3 0.7 copy.23
  (10 shorter events, 0.0 us)
Async XLA Ops:
  7.2 172.0 %all-gather.2.cloned.1.call-start = ((), (), s32[]{:S(2)}) async-start(), calls=%async_computation | async-start | bytes 9437184 | tf_op jit(solution)/shard_map/all_gather | solution.py:462
  84.2 26.9 %copy-start = (bf16[1,512,1024]{2,1,0:T(8,128)(2,1)S(1)}, bf16[1,512,1024]{2,1,0:T(8,128)(2,1)}, u32[]{:S(2)}) copy-start(bf16[1,512,1024]{2,1,0:T(8,128)(2,1)} %param.13) | copy-start | bytes 3145732
  114.0 63.5 %copy-start.2 = (s32[128]{0:T(128)S(1)}, s32[128]{0:T(128)}, u32[]{:S(2)}) copy-start(s32[128]{0:T(128)} %reshape_squeeze.3.far_s) | copy-start | bytes 1540
  114.0 63.6 %copy-start.3 = (s32[1,32]{1,0:T(1,128)S(1)}, s32[1,32]{1,0:T(1,128)}, u32[]{:S(2)}) copy-start(s32[1,32]{1,0:T(1,128)} %param.15) | copy-start | bytes 388
  179.1 39.2 %copy-start.1 = (f32[32,1024]{1,0:T(8,128)S(1)}, f32[32,1024]{1,0:T(8,128)}, u32[]{:S(2)}) copy-start(f32[32,1024]{1,0:T(8,128)} %get-tuple-element.56) | copy-start | bytes 393220
Sparse Core Ops, SparseCore 0:
  82.9 67.0 all-gather.1

commit v4 on v3

--- a/solution.py
+++ b/solution.py
@@ -13,6 +13,7 @@
 FAR = 4
 EPS = 1e-05
 CHUNKS = 4
+GROUP = 4
 SEQS, DPS = 8, 4
 SCALE = HEAD_DIM ** (-0.5)
 NT = (((1,), (1,)), ((), ()))
@@ -116,13 +117,22 @@
         for n in range(nb):
             at = pl.ds(pl.multiple_of(ki_s[r * nb + n] * BLK, BLK), BLK)
             on = (on_s[r * nb + n] > 0).astype(jnp.bfloat16)
-            for h in range(HEADS):
-                hs = slice(h * HEAD_DIM, (h + 1) * HEAD_DIM)
-                q, c = q_refs[n][:, hs], c_refs[n][:, hs] * on
-                act, der = silu_parts(dot(k_ref[at, hs], q, NT))
-                da = dot(v_ref[at, hs], c, NT)
-                dv_acc[at, hs] += dot(act.astype(jnp.bfloat16), c)
-                dk_acc[at, hs] += dot((da * der).astype(jnp.bfloat16), q)
+            for first in range(0, HEADS, GROUP):
+                cuts = [
+                    slice(h * HEAD_DIM, (h + 1) * HEAD_DIM) for h in range(first, first + GROUP)
+                ]
+                qs = [q_refs[n][:, hs] for hs in cuts]
+                cs = [c_refs[n][:, hs] * on for hs in cuts]
+                raw = [dot(k_ref[at, hs], q, NT) for hs, q in zip(cuts, qs)]
+                da = [dot(v_ref[at, hs], c, NT) for hs, c in zip(cuts, cs)]
+                act, der = silu_parts(jnp.concatenate(raw, axis=1))
+                ds = (jnp.concatenate(da, axis=1) * der).astype(jnp.bfloat16)
+                act = act.astype(jnp.bfloat16)
+                dv = [dot(act[:, g * BLK : (g + 1) * BLK], cs[g]) for g in range(GROUP)]
+                dk = [dot(ds[:, g * BLK : (g + 1) * BLK], qs[g]) for g in range(GROUP)]
+                wide = slice(first * HEAD_DIM, (first + GROUP) * HEAD_DIM)
+                dv_acc[at, wide] += jnp.concatenate(dv, axis=1)
+                dk_acc[at, wide] += jnp.concatenate(dk, axis=1)
 
     @pl.when(r == steps - 1)
     def _():
@@ -322,9 +332,12 @@
 
 
 def spread_kernel(count, *refs):
-    srcs, dsts = refs[:count], refs[count : 2 * count]
-    send, recv, own = refs[2 * count :]
+    srcs, later = refs[:count], refs[count]
+    dsts, later_out = refs[count + 1 : 2 * count + 1], refs[2 * count + 1]
+    send, recv, own = refs[2 * count + 2 :]
     greet(seq_peers())
+    passed = pltpu.make_async_copy(later, later_out, own.at[count])
+    passed.start()
     jobs = [
         Spread(srcs[a], dsts[a], send.at[a], recv.at[a], own.at[a]) for a in range(count)
     ]
@@ -336,26 +349,27 @@
         job.finish()
     for job in jobs:
         job.drain()
-
-
-def spread(arrays, ident):
+    passed.wait()
+
+
+def spread(arrays, later, ident):
     count = len(arrays)
     rows, width = arrays[0].shape
     anywhere = pl.BlockSpec(memory_space=pl.ANY)
     full = jax.ShapeDtypeStruct((SEQS * rows, width), jnp.bfloat16)
     return pl.pallas_call(
         functools.partial(spread_kernel, count),
-        out_shape=(full,) * count,
-        in_specs=[anywhere] * count,
-        out_specs=(anywhere,) * count,
+        out_shape=(full,) * count + (jax.ShapeDtypeStruct(later.shape, later.dtype),),
+        in_specs=[anywhere] * (count + 1),
+        out_specs=(anywhere,) * (count + 1),
         scratch_shapes=[
             pltpu.SemaphoreType.DMA((count, 7, CHUNKS)),
             pltpu.SemaphoreType.DMA((count, 7, CHUNKS)),
-            pltpu.SemaphoreType.DMA((count,)),
+            pltpu.SemaphoreType.DMA((count + 1,)),
         ],
         compiler_params=pltpu.CompilerParams(collective_id=ident, has_side_effects=True, vmem_limit_bytes=60 * 2**20),
         name="spread_rows",
-    )(*arrays)
+    )(*arrays, later)
 
 
 def tail_kernel(
@@ -472,8 +486,7 @@
     seqs, dps = lax.axis_size("seq"), lax.axis_size("dp")
     direct = (seqs, dps) == (SEQS, DPS)
     if direct:
-        k_all, v_all = spread([k, v], 1)
-        q_late, k_all, v_all = lax.optimization_barrier((q, k_all, v_all))
+        k_all, v_all, q_late = spread([k, v], q, 1)
         q_all = gather(q_late)
     else:
         k_all, v_all, q_all = gather(k), gather(v), gather(q)

time: 226 us -> 237 us (1.049)
  Pallas kernels: 202 us -> 214 us
    pallas_call x1, Pallas kernels: 75.5 us -> 101 us  [spread(): pl.pallas_call(functools.partial(spread_kernel, count), out_shape=(full,)...]
    pallas_call x1, Pallas kernels: 39.1 us -> 25.2 us  [run_keys(): pl.pallas_call(functools.partial(key_kernel, nb, steps), out_shape=(big,...]
  transfers between devices with their start and end apart: 1 -> 1, of which waited for: 0 -> 0; matrix products, arithmetic and copies ran while one was open for 4% -> 3% of each run, Pallas kernels for 39% -> 37%
where the time goes in v4:
time: 237 us
  Pallas kernels  214 us (90%)
  between operations  14.1 us (6%)
  other arithmetic  3 us (1%)
  local copies, waits for them, and re-layouts  2.99 us (1%)
  matrix products  2.83 us (1%)
    pallas_call x1, Pallas kernels, spread(): pl.pallas_call(functools.partial(spread_kernel, count), out_shape=(full,)...  101 us
    pallas_call x1, Pallas kernels, tail(): pl.pallas_call(tail_kernel, out_shape=(jax.ShapeDtypeStruct((SEQS * rows,...  60.2 us
    pallas_call x1, Pallas kernels, run_query(): pl.pallas_call(functools.partial(query_kernel, nb), out_shape=(big, big,...  26.9 us
    pallas_call x1, Pallas kernels, run_keys(): pl.pallas_call(functools.partial(key_kernel, nb, steps), out_shape=(big,...  25.2 us
  transfers between devices with their start and end apart: 1, of which 0 were waited for; matrix products, arithmetic and copies ran while one was open for 3% of the time, Pallas kernels for 37%

profile of v4, /device:TPU:0, one launch (start us, length us, event | category | flops | bytes accessed | tf_op | source)
XLA Modules:
  0.0 236.7 jit_solution(12868145171795825231)
XLA Ops:
  7.2 0.0 copy-start.2
  7.2 0.0 all-gather.2.cloned.1.call-start
  7.2 101.4 %spread_rows.1 = (bf16[4096,1024]{1,0:T(8,128)(2,1)}, bf16[4096,1024]{1,0:T(8,128)(2,1)}, bf16[512,1024]{1,0:T(8,128)(2,1)}) custom-call(bf16[512,1024]{1,0:T(8,128)(2,1)} %bitcast.20, bf16[512,1024]{1,0:T(8,128)(2,1)} %bitcast.23, bf16[512,1024]{1,0:T(8,128)(2,1)} %bitcast.27), custom_call_target="tpu_custom_call" | custom-call | tf_op jit(solution)/shard_map/spread_rows/pallas_call | solution.py:360
  108.6 0.0 all-gather.2.cloned.1.call-update
  108.6 0.0 copy-done.2
  108.7 0.1 copy.20
  108.7 0.7 reshape_squeeze.3.far_s
  109.4 26.9 %query_side.1 = (bf16[512,1024]{1,0:T(8,128)(2,1)}, bf16[512,1024]{1,0:T(8,128)(2,1)}, bf16[512,1024]{1,0:T(8,128)(2,1)}, bf16[512,1024]{1,0:T(8,128)(2,1)}, bf1...) custom-call(s32[128]{0:T(128)} %reshape_squeeze.3.far_s, s32[32]{0:T(128)} %bitcast.33, s32[1]{0:T(128)} %bitcast.1.my_s, ...), custom_call_target="tpu_custom_call" | custom-call | flops 8000000000 | bytes 25165824 | tf_op jit(solution)/shard_map/query_side/pallas_call | solution.py:162
  136.4 0.0 copy-done
  136.4 2.8 %convolution_convert_fusion = bf16[1024,1024]{1,0:T(8,128)(2,1)S(1)} fusion(bf16[512,1024]{1,0:T(8,128)(2,1)} %get-tuple-element.27, bf16[1,512,1024]{2,1,0:T(8,128)(2,1)S(1)} %copy-done), kind=kOutput, calls=%fused_computation | convolution fusion | flops 1074790400 | bytes 4194304 | tf_op jit(solution)/shard_map/dot_general | solution.py:24
  139.2 0.0 copy-start.3
  139.2 0.0 copy-start.4
  139.2 1.5 copy.21
  140.8 60.2 %tail_exchange.1 = (bf16[4096,1024]{1,0:T(8,128)(2,1)}, f32[32,1024]{1,0:T(8,128)}, f32[8,1024]{1,0:T(8,128)}) custom-call(bf16[512,1024]{1,0:T(8,128)(2,1)} %get-tuple-element.26.c_ref, bf16[2,4,128,1024]{3,2,1,0:T(8,128)(2,1)} %bitcast.26, f32[8,1024]{1,0:T(8,128)} %get-tuple-element.28.dg_ref), custom_call_target="tpu_custom_call" | custom-call | tf_op jit(solution)/shard_map/tail_exchange/pallas_call | solution.py:444
  200.9 1.4 reduce_sum.59
  202.3 0.0 copy-done.3
  202.4 0.1 convert_reduce_fusion
  202.5 0.0 copy-done.4
  202.5 0.1 select_reduce_fusion
  202.6 0.1 select_reduce_fusion.1
  202.7 0.7 pad_add_fusion.2.on_s
  203.4 0.6 pad_add_fusion
  204.0 25.2 %key_side.1 = (bf16[512,1024]{1,0:T(8,128)(2,1)}, bf16[512,1024]{1,0:T(8,128)(2,1)}) custom-call(s32[24]{0:T(128)} %get-tuple-element.38.qi_s, s32[24]{0:T(128)} %get-tuple-element.39.ki_s, s32[24]{0:T(128)} %pad_add_fusion.2.on_s, bf16[4096,1024]{1,0:T(8,128)(2,1)} %all-gather.2.cloned.1.call-done.refs_0_.refs_1_.refs_2_.refs_3_, ...), custom_call_target="tpu_custom_call" | custom-call | flops 4000000000 | bytes 16777216 | tf_op jit(solution)/shard_map/key_side/pallas_call | solution.py:196
  229.2 0.7 copy.23
  (12 shorter events, 0.1 us)
Async XLA Ops:
  7.2 101.5 %copy-start.2 = (s32[1,32,4]{1,2,0:T(4,128)S(1)}, s32[1,32,4]{1,2,0:T(4,128)}, u32[]{:S(2)}) copy-start(s32[1,32,4]{1,2,0:T(4,128)} %param.14) | copy-start | bytes 1540
  7.2 196.8 %all-gather.2.cloned.1.call-start = ((), (), s32[]{:S(2)}) async-start(), calls=%async_computation | async-start | bytes 9437184 | tf_op jit(solution)/shard_map/all_gather | solution.py:476
  109.4 26.9 %copy-start = (bf16[1,512,1024]{2,1,0:T(8,128)(2,1)S(1)}, bf16[1,512,1024]{2,1,0:T(8,128)(2,1)}, u32[]{:S(2)}) copy-start(bf16[1,512,1024]{2,1,0:T(8,128)(2,1)} %param.13) | copy-start | bytes 3145732
  139.2 63.1 %copy-start.3 = (s32[128]{0:T(128)S(1)}, s32[128]{0:T(128)}, u32[]{:S(2)}) copy-start(s32[128]{0:T(128)} %reshape_squeeze.3.far_s) | copy-start | bytes 1540
  139.2 63.2 %copy-start.4 = (s32[1,32]{1,0:T(1,128)S(1)}, s32[1,32]{1,0:T(1,128)}, u32[]{:S(2)}) copy-start(s32[1,32]{1,0:T(1,128)} %param.15) | copy-start | bytes 388
  204.0 25.2 %copy-start.1 = (f32[32,1024]{1,0:T(8,128)S(1)}, f32[32,1024]{1,0:T(8,128)}, u32[]{:S(2)}) copy-start(f32[32,1024]{1,0:T(8,128)} %get-tuple-element.52) | copy-start | bytes 393220
Sparse Core Ops, SparseCore 0:
  108.8 67.4 all-gather.1

commit v5 on v4

--- a/solution.py
+++ b/solution.py
@@ -332,12 +332,9 @@
 
 
 def spread_kernel(count, *refs):
-    srcs, later = refs[:count], refs[count]
-    dsts, later_out = refs[count + 1 : 2 * count + 1], refs[2 * count + 1]
-    send, recv, own = refs[2 * count + 2 :]
+    srcs, dsts = refs[:count], refs[count : 2 * count]
+    send, recv, own = refs[2 * count :]
     greet(seq_peers())
-    passed = pltpu.make_async_copy(later, later_out, own.at[count])
-    passed.start()
     jobs = [
         Spread(srcs[a], dsts[a], send.at[a], recv.at[a], own.at[a]) for a in range(count)
     ]
@@ -349,27 +346,26 @@
         job.finish()
     for job in jobs:
         job.drain()
-    passed.wait()
-
-
-def spread(arrays, later, ident):
+
+
+def spread(arrays, ident):
     count = len(arrays)
     rows, width = arrays[0].shape
     anywhere = pl.BlockSpec(memory_space=pl.ANY)
     full = jax.ShapeDtypeStruct((SEQS * rows, width), jnp.bfloat16)
     return pl.pallas_call(
         functools.partial(spread_kernel, count),
-        out_shape=(full,) * count + (jax.ShapeDtypeStruct(later.shape, later.dtype),),
-        in_specs=[anywhere] * (count + 1),
-        out_specs=(anywhere,) * (count + 1),
+        out_shape=(full,) * count,
+        in_specs=[pl.BlockSpec(memory_space=pltpu.VMEM)] * count,
+        out_specs=(anywhere,) * count,
         scratch_shapes=[
             pltpu.SemaphoreType.DMA((count, 7, CHUNKS)),
             pltpu.SemaphoreType.DMA((count, 7, CHUNKS)),
-            pltpu.SemaphoreType.DMA((count + 1,)),
+            pltpu.SemaphoreType.DMA((count,)),
         ],
         compiler_params=pltpu.CompilerParams(collective_id=ident, has_side_effects=True, vmem_limit_bytes=60 * 2**20),
         name="spread_rows",
-    )(*arrays, later)
+    )(*arrays)
 
 
 def tail_kernel(
@@ -448,7 +444,7 @@
             jax.ShapeDtypeStruct((depth, width), jnp.float32),
             jax.ShapeDtypeStruct(dg.shape, jnp.float32),
         ),
-        in_specs=[anywhere, vmem, vmem],
+        in_specs=[vmem, vmem, vmem],
         out_specs=(anywhere, vmem, vmem),
         scratch_shapes=[
             pltpu.VMEM((DPS, part, width), b16),
@@ -486,7 +482,8 @@
     seqs, dps = lax.axis_size("seq"), lax.axis_size("dp")
     direct = (seqs, dps) == (SEQS, DPS)
     if direct:
-        k_all, v_all, q_late = spread([k, v], q, 1)
+        k_all, v_all = spread([k, v], 1)
+        q_late, k_all, v_all = lax.optimization_barrier((q, k_all, v_all))
         q_all = gather(q_late)
     else:
         k_all, v_all, q_all = gather(k), gather(v), gather(q)

time: 237 us -> 213 us (0.90)
  Pallas kernels: 214 us -> 189 us
    pallas_call x1, Pallas kernels: 101 us -> 76.8 us  [spread(): pl.pallas_call(functools.partial(spread_kernel, count), out_shape=(full,)...]
  transfers between devices with their start and end apart: 1 -> 1, of which waited for: 0 -> 0; matrix products, arithmetic and copies ran while one was open for 3% -> 4% of each run, Pallas kernels for 37% -> 41%
where the time goes in v5:
time: 213 us
  Pallas kernels  189 us (89%)
  between operations  14.1 us (7%)
  local copies, waits for them, and re-layouts  3.6 us (2%)
  other arithmetic  3 us (1%)
  matrix products  2.83 us (1%)
    pallas_call x1, Pallas kernels, spread(): pl.pallas_call(functools.partial(spread_kernel, count), out_shape=(full,)...  76.8 us
    pallas_call x1, Pallas kernels, tail(): pl.pallas_call(tail_kernel, out_shape=(jax.ShapeDtypeStruct((SEQS * rows,...  60.5 us
    pallas_call x1, Pallas kernels, run_query(): pl.pallas_call(functools.partial(query_kernel, nb), out_shape=(big, big,...  26.9 us
    pallas_call x1, Pallas kernels, run_keys(): pl.pallas_call(functools.partial(key_kernel, nb, steps), out_shape=(big,...  25.2 us
  transfers between devices with their start and end apart: 1, of which 0 were waited for; matrix products, arithmetic and copies ran while one was open for 4% of the time, Pallas kernels for 41%

profile of v5, /device:TPU:0, one launch (start us, length us, event | category | flops | bytes accessed | tf_op | source)
XLA Modules:
  0.0 213.1 jit_solution(4915514975758245327)
XLA Ops:
  7.2 0.0 all-gather.2.cloned.1.call-start
  7.2 76.8 %spread_rows.1 = (bf16[4096,1024]{1,0:T(8,128)(2,1)}, bf16[4096,1024]{1,0:T(8,128)(2,1)}) custom-call(bf16[512,1024]{1,0:T(8,128)(2,1)} %bitcast.20, bf16[512,1024]{1,0:T(8,128)(2,1)} %bitcast.23), custom_call_target="tpu_custom_call" | custom-call | tf_op jit(solution)/shard_map/spread_rows/pallas_call | solution.py:356
  84.1 0.0 all-gather.2.cloned.1.call-update
  84.1 0.8 copy.20
  84.9 0.6 reshape_squeeze.3.far_s
  85.5 0.0 copy-start
  85.5 26.9 %query_side.1 = (bf16[512,1024]{1,0:T(8,128)(2,1)}, bf16[512,1024]{1,0:T(8,128)(2,1)}, bf16[512,1024]{1,0:T(8,128)(2,1)}, bf16[512,1024]{1,0:T(8,128)(2,1)}, bf1...) custom-call(s32[128]{0:T(128)} %reshape_squeeze.3.far_s, s32[32]{0:T(128)} %bitcast.33, s32[1]{0:T(128)} %bitcast.1.my_s, ...), custom_call_target="tpu_custom_call" | custom-call | flops 8000000000 | bytes 25165824 | tf_op jit(solution)/shard_map/query_side/pallas_call | solution.py:162
  112.4 0.0 copy-done
  112.4 2.8 %convolution_convert_fusion = bf16[1024,1024]{1,0:T(8,128)(2,1)S(1)} fusion(bf16[512,1024]{1,0:T(8,128)(2,1)} %get-tuple-element.31, bf16[1,512,1024]{2,1,0:T(8,128)(2,1)S(1)} %copy-done), kind=kOutput, calls=%fused_computation | convolution fusion | flops 1074790400 | bytes 4194304 | tf_op jit(solution)/shard_map/dot_general | solution.py:24
  115.2 0.0 copy-start.2
  115.3 0.0 copy-start.3
  115.3 1.5 copy.21
  116.8 60.5 %tail_exchange.1 = (bf16[4096,1024]{1,0:T(8,128)(2,1)}, f32[32,1024]{1,0:T(8,128)}, f32[8,1024]{1,0:T(8,128)}) custom-call(bf16[512,1024]{1,0:T(8,128)(2,1)} %get-tuple-element.30.c_ref, bf16[2,4,128,1024]{3,2,1,0:T(8,128)(2,1)} %bitcast.26, f32[8,1024]{1,0:T(8,128)} %get-tuple-element.32.dg_ref), custom_call_target="tpu_custom_call" | custom-call | tf_op jit(solution)/shard_map/tail_exchange/pallas_call | solution.py:440
  177.3 1.4 reduce_sum.59
  178.7 0.0 copy-done.2
  178.8 0.1 convert_reduce_fusion
  178.9 0.0 copy-done.3
  178.9 0.1 select_reduce_fusion
  179.0 0.1 select_reduce_fusion.1
  179.1 0.7 pad_add_fusion.2.on_s
  179.8 0.6 pad_add_fusion
  180.4 25.2 %key_side.1 = (bf16[512,1024]{1,0:T(8,128)(2,1)}, bf16[512,1024]{1,0:T(8,128)(2,1)}) custom-call(s32[24]{0:T(128)} %get-tuple-element.42.qi_s, s32[24]{0:T(128)} %get-tuple-element.43.ki_s, s32[24]{0:T(128)} %pad_add_fusion.2.on_s, bf16[4096,1024]{1,0:T(8,128)(2,1)} %all-gather.2.cloned.1.call-done.refs_0_.refs_1_.refs_2_.refs_3_, ...), custom_call_target="tpu_custom_call" | custom-call | flops 4000000000 | bytes 16777216 | tf_op jit(solution)/shard_map/key_side/pallas_call | solution.py:196
  205.6 0.0 copy-done.1
  205.6 0.7 copy.23
  (10 shorter events, 0.0 us)
Async XLA Ops:
  7.2 173.2 %all-gather.2.cloned.1.call-start = ((), (), s32[]{:S(2)}) async-start(), calls=%async_computation | async-start | bytes 9437184 | tf_op jit(solution)/shard_map/all_gather | solution.py:472
  85.5 26.9 %copy-start = (bf16[1,512,1024]{2,1,0:T(8,128)(2,1)S(1)}, bf16[1,512,1024]{2,1,0:T(8,128)(2,1)}, u32[]{:S(2)}) copy-start(bf16[1,512,1024]{2,1,0:T(8,128)(2,1)} %param.13) | copy-start | bytes 3145732
  115.2 63.5 %copy-start.2 = (s32[128]{0:T(128)S(1)}, s32[128]{0:T(128)}, u32[]{:S(2)}) copy-start(s32[128]{0:T(128)} %reshape_squeeze.3.far_s) | copy-start | bytes 1540
  115.3 63.6 %copy-start.3 = (s32[1,32]{1,0:T(1,128)S(1)}, s32[1,32]{1,0:T(1,128)}, u32[]{:S(2)}) copy-start(s32[1,32]{1,0:T(1,128)} %param.15) | copy-start | bytes 388
  180.4 25.2 %copy-start.1 = (f32[32,1024]{1,0:T(8,128)S(1)}, f32[32,1024]{1,0:T(8,128)}, u32[]{:S(2)}) copy-start(f32[32,1024]{1,0:T(8,128)} %get-tuple-element.56) | copy-start | bytes 393220
Sparse Core Ops, SparseCore 0:
  84.2 67.0 all-gather.1
